TPU v7x, 128 devices: a whole 4x4x4 slice. The times are simulated.
128 devices in a mesh: dp: 64 (over y, z_hi, x, core), head: 2 (over z_lo).
Axes of the slice: x: 4, y: 4, z: 4 (z_hi: 2, z_lo: 2; z = z_hi * 2 + z_lo), core: 2. Of those that a mesh axis runs over, the one named last changes fastest.
Arguments:
- decoder_in: bfloat16 [16384, 768], P('dp'), may hold values from -6 to 6
- encoder_states: bfloat16 [8192, 768], P('dp'), may hold values from -6 to 6
- keep_mask: int32 [8192], P('dp'), may hold values from 0 to 1, as said below
- selection: int32 [16384, 1024], P('dp'), may hold values from 0 to 8191, as said below
- self_proj: bfloat16 [3, 768, 768], P(None, None, 'head'), may hold values from -0.21875 to 0.21875
- self_bias: bfloat16 [2, 768], P(None, 'head'), may hold values from -3 to 3
- self_out: bfloat16 [768, 768], P('head'), may hold values from -1.25 to 1.25
- self_out_bias: bfloat16 [768], replicated, may hold values from -3 to 3
- norm1_gain: bfloat16 [768], replicated, may hold values from 0.5 to 1.5
- norm1_bias: bfloat16 [768], replicated, may hold values from -3 to 3
- cross_query: bfloat16 [768, 768], P(None, 'head'), may hold values from -0.21875 to 0.21875
- cross_memory: bfloat16 [2, 768, 768], P(None, None, 'head'), may hold values from -0.21875 to 0.21875
- cross_bias: bfloat16 [2, 768], P(None, 'head'), may hold values from -3 to 3
- cross_out: bfloat16 [768, 768], P('head'), may hold values from -3.5 to 3.5
- cross_out_bias: bfloat16 [768], replicated, may hold values from -3 to 3
- norm2_gain: bfloat16 [768], replicated, may hold values from 0.5 to 1.5
- norm2_bias: bfloat16 [768], replicated, may hold values from -3 to 3
- expand_weight: bfloat16 [768, 3072], P(None, 'head'), may hold values from -0.21875 to 0.21875
- expand_bias: bfloat16 [3072], P('head'), may hold values from -3 to 3
- reduce_weight: bfloat16 [3072, 768], P('head'), may hold values from -0.109375 to 0.109375
- reduce_bias: bfloat16 [768], replicated, may hold values from -3 to 3
- norm3_gain: bfloat16 [768], replicated, may hold values from 0.5 to 1.5
- norm3_bias: bfloat16 [768], replicated, may hold values from -3 to 3
- out_cotangent: bfloat16 [16384, 768], P('dp'), may hold values from -6 to 6
Outputs:
- layer_out: bfloat16 [16384, 768], P('dp')
- input_grad: float32 [16384, 768], P('dp')
- grad_self_proj: float32 [3, 768, 768], P(None, None, 'head')
- grad_self_bias: float32 [2, 768], P(None, 'head')
- grad_self_out: float32 [768, 768], P('head')
- grad_self_out_bias: float32 [768], replicated
- grad_norm1_gain: float32 [768], replicated
- grad_norm1_bias: float32 [768], replicated
- grad_cross_query: float32 [768, 768], P(None, 'head')
- grad_cross_memory: float32 [2, 768, 768], P(None, None, 'head')
- grad_cross_bias: float32 [2, 768], P(None, 'head')
- grad_cross_out: float32 [768, 768], P('head')
- grad_cross_out_bias: float32 [768], replicated
- grad_norm2_gain: float32 [768], replicated
- grad_norm2_bias: float32 [768], replicated
- grad_expand: float32 [768, 3072], P(None, 'head')
- grad_expand_bias: float32 [3072], P('head')
- grad_reduce: float32 [3072, 768], P('head')
- grad_reduce_bias: float32 [768], replicated
- grad_norm3_gain: float32 [768], replicated
- grad_norm3_bias: float32 [768], replicated
Inputs may be any that keep to these rules, and one draw needn't show every extreme that they name: `selection`: each row names 1024 encoder states by their place among all 8192; repeats may occur. Some tokens retrieve only states whose keep_mask is 0. `keep_mask`: each block of 128 consecutive states is one encoder group. Its middle half is kept; its first quarter is kept where a document begins in that group, its last quarter where a document ends there; a document that ends in one group is followed by one that begins in the next. The first group begins a document that goes on into the second group; the last group ends one.
All inputs are finite; a program needn't handle non-finite values.
Results may differ from a plain program's by a relative error of at most 0.035.
Values may be sent and summed in bfloat16 or wider, within the bound.
No kernel may reach another device: no remote copies, remote signals or barrier semaphores. Data moves between devices by JAX's collectives and lax.ppermute only.
A program may use at most 192 MiB of HBM per device.

v0:
```python
import math

import jax
import jax.numpy as jnp
from jax import lax
from jax.sharding import PartitionSpec as P

HEAD_DIM = 64


masked_score = -1e30
epsilon = 1e-05


def layer_norm(token_rows, norm_gain, norm_bias):
    row_mean = jnp.mean(token_rows, axis=-1, keepdims=True)
    centered = token_rows - row_mean
    variance = jnp.mean(centered * centered, axis=-1, keepdims=True)
    inverse = lax.rsqrt(variance + epsilon)
    normed = centered * inverse
    return (normed * norm_gain.astype(jnp.float32) + norm_bias.astype(jnp.float32), normed, inverse)


def norm_back(upstream, normed, inverse, norm_gain):
    scaled = upstream * norm_gain.astype(jnp.float32)
    mean_one = jnp.mean(scaled, axis=-1, keepdims=True)
    mean_two = jnp.mean(scaled * normed, axis=-1, keepdims=True)
    return (
        inverse * (scaled - mean_one - normed * mean_two),
        jnp.sum(upstream * normed, axis=0),
        jnp.sum(upstream, axis=0),
    )


def split_heads(flat_rows):
    return flat_rows.reshape(flat_rows.shape[0], flat_rows.shape[1] // HEAD_DIM, HEAD_DIM)


def exact_gelu(values):
    return jax.nn.gelu(values, approximate=False)


def selection_table(selection, total_states):
    low_width = math.gcd(total_states, 128)
    high_count = total_states // low_width
    high_part = selection // low_width
    low_part = selection - high_part * low_width
    high_hot = (high_part[..., None] == jnp.arange(high_count, dtype=jnp.int32)).astype(
        jnp.bfloat16
    )
    low_hot = (low_part[..., None] == jnp.arange(low_width, dtype=jnp.int32)).astype(jnp.bfloat16)
    counts = jnp.einsum("tkh,tkl->thl", high_hot, low_hot, preferred_element_type=jnp.float32)
    return (counts > 0.5).astype(jnp.bfloat16).reshape(selection.shape[0], total_states)


def whole_memory(key_rows, value_rows, keep_rows):
    return (
        lax.all_gather(key_rows, "dp", axis=0, tiled=True),
        lax.all_gather(value_rows, "dp", axis=0, tiled=True),
        lax.all_gather(keep_rows, "dp", axis=0, tiled=True),
    )


def online_step(queries3, chosen):
    scale_factor = HEAD_DIM ** (-0.5)

    def absorb(running, shard_piece, offset):
        key_piece, value_piece, keep_piece = shard_piece
        piece_rows = key_piece.shape[0]
        block_len = math.gcd(piece_rows, 1024)

        def one_block(turn_index, running_state):
            running_max, running_sum, running_out = running_state
            first_key = turn_index * block_len
            key_block = lax.dynamic_slice_in_dim(key_piece, first_key, block_len, 0)
            value_block = lax.dynamic_slice_in_dim(value_piece, first_key, block_len, 0)
            keep_block = lax.dynamic_slice_in_dim(keep_piece, first_key, block_len, 0)
            picked = lax.dynamic_slice_in_dim(chosen, first_key, block_len, 1)
            allowed = picked * keep_block[None, :] > 0.5
            scores = (
                jnp.einsum(
                    "qhd,khd->hqk",
                    queries3,
                    split_heads(key_block),
                    preferred_element_type=jnp.float32,
                )
                * scale_factor
            )
            scores = jnp.where(allowed[None], scores, masked_score)
            new_max = jnp.maximum(running_max, jnp.max(scores, axis=-1))
            shrink = jnp.exp(running_max - new_max)
            powers = jnp.exp(scores - new_max[..., None])
            new_sum = running_sum * shrink + jnp.sum(powers, axis=-1)
            new_out = running_out * shrink[..., None] + jnp.einsum(
                "hqk,khd->hqd",
                powers.astype(jnp.bfloat16),
                split_heads(value_block),
                preferred_element_type=jnp.float32,
            )
            return (new_max, new_sum, new_out)

        return lax.fori_loop(0, piece_rows // block_len, one_block, running)

    return absorb


def shards(
    decoder_in,
    encoder_states,
    keep_mask,
    selection,
    self_proj,
    self_bias,
    self_out,
    self_out_bias,
    norm1_gain,
    norm1_bias,
    cross_query,
    cross_memory,
    cross_bias,
    cross_out,
    cross_out_bias,
    norm2_gain,
    norm2_bias,
    expand_weight,
    expand_bias,
    reduce_weight,
    reduce_bias,
    norm3_gain,
    norm3_bias,
    out_cotangent,
):
    tokens_here = decoder_in.shape[0]
    scale_factor = HEAD_DIM ** (-0.5)
    inputs = decoder_in.astype(jnp.float32)
    positions = jnp.arange(tokens_here, dtype=jnp.int32)
    causal = positions[:, None] >= positions[None, :]
    projected = jnp.einsum("sd,kde->kse", decoder_in, self_proj, preferred_element_type=jnp.float32)
    bias_rows = self_bias.astype(jnp.float32)
    self_queries = (projected[0] + bias_rows[0]).astype(jnp.bfloat16)
    self_keys = projected[1].astype(jnp.bfloat16)
    self_values = (projected[2] + bias_rows[1]).astype(jnp.bfloat16)
    query_heads = split_heads(self_queries)
    key_heads = split_heads(self_keys)
    value_heads = split_heads(self_values)
    self_scores = (
        jnp.einsum("qhd,khd->hqk", query_heads, key_heads, preferred_element_type=jnp.float32)
        * scale_factor
    )
    self_scores = jnp.where(causal[None], self_scores, masked_score)
    self_attn = jax.nn.softmax(self_scores, axis=-1)
    self_attn_low = self_attn.astype(jnp.bfloat16)
    self_mixed = (
        jnp.einsum("hqk,khd->qhd", self_attn_low, value_heads, preferred_element_type=jnp.float32)
        .reshape(tokens_here, -1)
        .astype(jnp.bfloat16)
    )
    self_part = jnp.dot(self_mixed, self_out, preferred_element_type=jnp.float32)
    self_total = lax.psum(self_part.astype(jnp.bfloat16), "head").astype(jnp.float32)
    after_self, normed1, inverse1 = layer_norm(
        inputs + self_total + self_out_bias.astype(jnp.float32), norm1_gain, norm1_bias
    )
    after_self_low = after_self.astype(jnp.bfloat16)
    cross_rows = cross_bias.astype(jnp.float32)
    cross_queries = (
        jnp.dot(after_self_low, cross_query, preferred_element_type=jnp.float32) + cross_rows[0]
    ).astype(jnp.bfloat16)
    memory = jnp.einsum(
        "ed,kdf->kef", encoder_states, cross_memory, preferred_element_type=jnp.float32
    )
    cross_keys = memory[0].astype(jnp.bfloat16)
    cross_values = (memory[1] + cross_rows[1]).astype(jnp.bfloat16)
    keep_low = keep_mask.astype(jnp.bfloat16)
    total_states = encoder_states.shape[0] * lax.axis_size("dp")
    chosen = selection_table(selection, total_states)
    queries3 = split_heads(cross_queries)
    heads_here = queries3.shape[1]
    start_state = (
        jnp.full((heads_here, tokens_here), masked_score, jnp.float32),
        jnp.zeros((heads_here, tokens_here), jnp.float32),
        jnp.zeros((heads_here, tokens_here, HEAD_DIM), jnp.float32),
    )
    absorb = online_step(queries3, chosen)
    folded = absorb(
        start_state,
        (
            lax.all_gather(cross_keys, "dp", axis=0, tiled=True),
            lax.all_gather(cross_values, "dp", axis=0, tiled=True),
            lax.all_gather(keep_low, "dp", axis=0, tiled=True),
        ),
        jnp.int32(0),
    )
    running_max, running_sum, running_out = folded
    recalled_full = jnp.transpose(running_out / running_sum[..., None], (1, 0, 2))
    recalled = recalled_full.reshape(tokens_here, -1).astype(jnp.bfloat16)
    cross_part = jnp.dot(recalled, cross_out, preferred_element_type=jnp.float32)
    cross_total = lax.psum(cross_part.astype(jnp.bfloat16), "head").astype(jnp.float32)
    after_cross, normed2, inverse2 = layer_norm(
        after_self + cross_total + cross_out_bias.astype(jnp.float32), norm2_gain, norm2_bias
    )
    after_cross_low = after_cross.astype(jnp.bfloat16)
    expanded = jnp.dot(
        after_cross_low, expand_weight, preferred_element_type=jnp.float32
    ) + expand_bias.astype(jnp.float32)
    activated, gelu_back = jax.vjp(exact_gelu, expanded)
    hidden = activated.astype(jnp.bfloat16)
    reduce_part = jnp.dot(hidden, reduce_weight, preferred_element_type=jnp.float32)
    reduce_total = lax.psum(reduce_part.astype(jnp.bfloat16), "head").astype(jnp.float32)
    output_rows, normed3, inverse3 = layer_norm(
        after_cross + reduce_total + reduce_bias.astype(jnp.float32), norm3_gain, norm3_bias
    )
    layer_out = output_rows.astype(jnp.bfloat16)
    upstream = out_cotangent.astype(jnp.float32)
    grad_r3, grad_norm3_gain, grad_norm3_bias = norm_back(upstream, normed3, inverse3, norm3_gain)
    grad_reduce_bias = jnp.sum(grad_r3, axis=0)
    grad_r3_low = grad_r3.astype(jnp.bfloat16)
    grad_reduce = jnp.einsum("sf,sd->fd", hidden, grad_r3_low, preferred_element_type=jnp.float32)
    grad_hidden = jnp.einsum(
        "sd,fd->sf", grad_r3_low, reduce_weight, preferred_element_type=jnp.float32
    ).astype(jnp.bfloat16)
    grad_expanded = gelu_back(grad_hidden.astype(jnp.float32))[0]
    grad_expand_bias = jnp.sum(grad_expanded, axis=0)
    grad_expanded_low = grad_expanded.astype(jnp.bfloat16)
    grad_expand = jnp.einsum(
        "sd,sf->df", after_cross_low, grad_expanded_low, preferred_element_type=jnp.float32
    )
    ffn_back_part = jnp.einsum(
        "sf,df->sd", grad_expanded_low, expand_weight, preferred_element_type=jnp.float32
    )
    grad_after_cross = grad_r3 + lax.psum(ffn_back_part.astype(jnp.bfloat16), "head").astype(
        jnp.float32
    )
    grad_r2, grad_norm2_gain, grad_norm2_bias = norm_back(
        grad_after_cross, normed2, inverse2, norm2_gain
    )
    grad_cross_out_bias = jnp.sum(grad_r2, axis=0)
    grad_r2_low = grad_r2.astype(jnp.bfloat16)
    grad_cross_out = jnp.einsum(
        "sk,sd->kd", recalled, grad_r2_low, preferred_element_type=jnp.float32
    )
    grad_recalled = jnp.einsum(
        "sd,kd->sk", grad_r2_low, cross_out, preferred_element_type=jnp.float32
    ).astype(jnp.bfloat16)
    grad_recalled3 = split_heads(grad_recalled)
    correction = jnp.transpose(jnp.sum(grad_recalled3.astype(jnp.float32) * recalled_full, axis=-1))
    full_keys, full_values, full_keep = whole_memory(cross_keys, cross_values, keep_low)
    block_len = math.gcd(total_states, 1024)

    def scan_step(query_grad, turn_index):
        first_key = turn_index * block_len
        key_block = split_heads(lax.dynamic_slice_in_dim(full_keys, first_key, block_len, 0))
        value_block = split_heads(lax.dynamic_slice_in_dim(full_values, first_key, block_len, 0))
        keep_block = lax.dynamic_slice_in_dim(full_keep, first_key, block_len, 0)
        picked = lax.dynamic_slice_in_dim(chosen, first_key, block_len, 1)
        allowed = picked * keep_block[None, :] > 0.5
        scores = (
            jnp.einsum("qhd,khd->hqk", queries3, key_block, preferred_element_type=jnp.float32)
            * scale_factor
        )
        scores = jnp.where(allowed[None], scores, masked_score)
        attn_weights = jnp.exp(scores - running_max[..., None]) / running_sum[..., None]
        attn_low = attn_weights.astype(jnp.bfloat16)
        grad_attn = jnp.einsum(
            "qhd,khd->hqk", grad_recalled3, value_block, preferred_element_type=jnp.float32
        )
        grad_scores = jnp.where(
            allowed[None], attn_weights * (grad_attn - correction[..., None]), 0.0
        ).astype(jnp.bfloat16)
        query_part = (
            jnp.einsum("hqk,khd->qhd", grad_scores, key_block, preferred_element_type=jnp.float32)
            * scale_factor
        )
        key_part = (
            jnp.einsum("hqk,qhd->khd", grad_scores, queries3, preferred_element_type=jnp.float32)
            * scale_factor
        )
        value_part = jnp.einsum(
            "hqk,qhd->khd", attn_low, grad_recalled3, preferred_element_type=jnp.float32
        )
        state_part = jnp.concatenate(
            [key_part.reshape(block_len, -1), value_part.reshape(block_len, -1)], axis=1
        )
        return (query_grad + query_part, state_part)

    query_grad, state_parts = lax.scan(
        scan_step,
        jnp.zeros((tokens_here, heads_here, HEAD_DIM), jnp.float32),
        jnp.arange(total_states // block_len, dtype=jnp.int32),
    )
    state_parts = state_parts.reshape(total_states, -1)
    width_here = cross_keys.shape[1]
    owned_grads = lax.psum_scatter(state_parts, "dp", scatter_dimension=0, tiled=True)
    grad_cross_memory = jnp.einsum(
        "ed,esk->sdk",
        encoder_states,
        owned_grads.reshape(-1, 2, width_here),
        precision=lax.Precision.HIGHEST,
        preferred_element_type=jnp.float32,
    )
    value_bias_grad = jnp.sum(owned_grads[:, width_here:], axis=0)
    grad_cross_queries = query_grad.reshape(tokens_here, -1).astype(jnp.bfloat16)
    grad_cross_bias = jnp.stack(
        [jnp.sum(grad_cross_queries.astype(jnp.float32), axis=0), value_bias_grad]
    )
    grad_cross_query = jnp.einsum(
        "sd,sk->dk", after_self_low, grad_cross_queries, preferred_element_type=jnp.float32
    )
    cross_back_part = jnp.einsum(
        "sk,dk->sd", grad_cross_queries, cross_query, preferred_element_type=jnp.float32
    )
    grad_after_self = grad_r2 + lax.psum(cross_back_part.astype(jnp.bfloat16), "head").astype(
        jnp.float32
    )
    grad_r1, grad_norm1_gain, grad_norm1_bias = norm_back(
        grad_after_self, normed1, inverse1, norm1_gain
    )
    grad_self_out_bias = jnp.sum(grad_r1, axis=0)
    grad_r1_low = grad_r1.astype(jnp.bfloat16)
    grad_self_out = jnp.einsum(
        "sk,sd->kd", self_mixed, grad_r1_low, preferred_element_type=jnp.float32
    )
    grad_mixed = jnp.einsum(
        "sd,kd->sk", grad_r1_low, self_out, preferred_element_type=jnp.float32
    ).astype(jnp.bfloat16)
    grad_mixed3 = split_heads(grad_mixed)
    grad_attn = jnp.einsum(
        "qhd,khd->hqk", grad_mixed3, value_heads, preferred_element_type=jnp.float32
    )
    row_correction = jnp.sum(self_attn * grad_attn, axis=-1, keepdims=True)
    grad_self_scores = (self_attn * (grad_attn - row_correction)).astype(jnp.bfloat16)
    grad_q = (
        (
            jnp.einsum(
                "hqk,khd->qhd", grad_self_scores, key_heads, preferred_element_type=jnp.float32
            )
            * scale_factor
        )
        .reshape(tokens_here, -1)
        .astype(jnp.bfloat16)
    )
    grad_k = (
        (
            jnp.einsum(
                "hqk,qhd->khd", grad_self_scores, query_heads, preferred_element_type=jnp.float32
            )
            * scale_factor
        )
        .reshape(tokens_here, -1)
        .astype(jnp.bfloat16)
    )
    grad_v = (
        jnp.einsum("hqk,qhd->khd", self_attn_low, grad_mixed3, preferred_element_type=jnp.float32)
        .reshape(tokens_here, -1)
        .astype(jnp.bfloat16)
    )
    grad_proj_rows = jnp.stack([grad_q, grad_k, grad_v])
    grad_self_proj = jnp.einsum(
        "sd,kse->kde", decoder_in, grad_proj_rows, preferred_element_type=jnp.float32
    )
    grad_self_bias = jnp.stack(
        [jnp.sum(grad_q.astype(jnp.float32), axis=0), jnp.sum(grad_v.astype(jnp.float32), axis=0)]
    )
    self_back_part = jnp.einsum(
        "kse,kde->sd", grad_proj_rows, self_proj, preferred_element_type=jnp.float32
    )
    input_grad = grad_r1 + lax.psum(self_back_part.astype(jnp.bfloat16), "head").astype(jnp.float32)
    (
        grad_self_proj,
        grad_self_bias,
        grad_self_out,
        grad_self_out_bias,
        grad_norm1_gain,
        grad_norm1_bias,
        grad_cross_query,
        grad_cross_memory,
        grad_cross_bias,
        grad_cross_out,
        grad_cross_out_bias,
        grad_norm2_gain,
        grad_norm2_bias,
        grad_expand,
        grad_expand_bias,
        grad_reduce,
        grad_reduce_bias,
        grad_norm3_gain,
        grad_norm3_bias,
    ) = lax.psum(
        (
            grad_self_proj,
            grad_self_bias,
            grad_self_out,
            grad_self_out_bias,
            grad_norm1_gain,
            grad_norm1_bias,
            grad_cross_query,
            grad_cross_memory,
            grad_cross_bias,
            grad_cross_out,
            grad_cross_out_bias,
            grad_norm2_gain,
            grad_norm2_bias,
            grad_expand,
            grad_expand_bias,
            grad_reduce,
            grad_reduce_bias,
            grad_norm3_gain,
            grad_norm3_bias,
        ),
        "dp",
    )
    return (
        layer_out,
        input_grad,
        grad_self_proj,
        grad_self_bias,
        grad_self_out,
        grad_self_out_bias,
        grad_norm1_gain,
        grad_norm1_bias,
        grad_cross_query,
        grad_cross_memory,
        grad_cross_bias,
        grad_cross_out,
        grad_cross_out_bias,
        grad_norm2_gain,
        grad_norm2_bias,
        grad_expand,
        grad_expand_bias,
        grad_reduce,
        grad_reduce_bias,
        grad_norm3_gain,
        grad_norm3_bias,
    )


def solution(mesh):
    in_specs = (
        P("dp", None),
        P("dp", None),
        P("dp"),
        P("dp", None),
        P(None, None, "head"),
        P(None, "head"),
        P("head", None),
        P(),
        P(),
        P(),
        P(None, "head"),
        P(None, None, "head"),
        P(None, "head"),
        P("head", None),
        P(),
        P(),
        P(),
        P(None, "head"),
        P("head"),
        P("head", None),
        P(),
        P(),
        P(),
        P("dp", None),
    )
    out_specs = (
        P("dp", None),
        P("dp", None),
        P(None, None, "head"),
        P(None, "head"),
        P("head", None),
        P(),
        P(),
        P(),
        P(None, "head"),
        P(None, None, "head"),
        P(None, "head"),
        P("head", None),
        P(),
        P(),
        P(),
        P(None, "head"),
        P("head"),
        P("head", None),
        P(),
        P(),
        P(),
    )
    return jax.shard_map(shards, mesh=mesh, in_specs=in_specs, out_specs=out_specs, check_vma=False)
```

profile of v0, /device:TPU:1, one launch (start us, length us, event | category | flops | bytes accessed | tf_op | source)
XLA Modules:
  0.0 1618.8 jit_solution(689894832131615546)
XLA Ops:
  21.6 10.1 iota_compare_fusion.15
  31.7 68.0 %compare_convert_fusion = bf16[256,64,128]{2,1,0:T(8,128)(2,1)} fusion(s32[256,1024]{1,0:T(8,128)S(1)} %get-tuple-element.553, pred[256,1024,64]{1,2,0:T(32,128)(4,1)S(1)} %iota_compare_fusion.15), kind=kOutput, calls=%fused_computation.42 | convolution fusion | flops 4332716032 | bytes 22020096 | tf_op jit(solution)/shard_map/tkh,tkl->thl/dot_general | solution.py:52
  99.7 7.0 copy.127
  106.8 97.9 %all-gather.1 = bf16[64,1,128]{2,1,0:T(2,128)(2,1)S(1)} all-gather(bf16[1,1,128]{2,1,0:T(2,128)(2,1)S(1)} %convert_bitcast_fusion), channel_id=1, replica_groups=mesh['dp'=64,'head'=2] {'dp'}, dimensions={0}, use_global_device_ids=true | all-gather | bytes 16640 | tf_op jit(solution)/shard_map/all_gather | solution.py:189
  210.2 131.7 %while.31 = (s32[]{:T(128)}, f32[6,256]{1,0:T(8,128)S(1)}, f32[6,256]{1,0:T(8,128)S(1)}, f32[6,256,64]{1,2,0:T(8,128)}, bf16[256,8192]{0,1:T(8,128)(2,1)}, /*ind...) while((s32[]{:T(128)}, f32[6,256]{1,0:T(8,128)S(1)}, ...), condition=%wide.region_8.9_spmd.clone, body=%wide.region_5.8_spmd.clone.sunk | while | flops 421568000 | bytes 51419364 | solution.py:102
  218.5 4.2 fusion.161
  234.9 4.2 fusion.161
  251.4 4.2 fusion.161
  267.8 4.2 fusion.161
  284.3 4.2 fusion.161
  296.9 3.9 fusion.160
  300.8 4.2 fusion.161
  317.2 4.2 fusion.161
  333.7 4.2 fusion.161
  348.1 23.5 %all-reduce.12.cloned.1.call-done = bf16[256,768]{1,0:T(8,128)(2,1)} async-done(((bf16[256,768]{1,0:T(8,128)(2,1)}), bf16[256,768]{1,0:T(8,128)(2,1)}) %all-reduce.12.cloned.1.call-update) | async-done | bytes 393232 | tf_op jit(solution)/shard_map/psum | solution.py:197
  373.5 5.2 multiply_convert_fusion.1
  385.1 29.7 %all-reduce.14.cloned.1.call-done = bf16[256,768]{1,0:T(8,128)(2,1)} async-done(((bf16[256,768]{1,0:T(8,128)(2,1)}), bf16[256,768]{1,0:T(8,128)(2,1)}) %all-reduce.14.cloned.1.call-update) | async-done | bytes 393232 | tf_op jit(solution)/shard_map/psum | solution.py:208
  423.1 33.3 %all-reduce.16.cloned.1.call-done = bf16[256,768]{1,0:T(8,128)(2,1)} async-done(((bf16[256,768]{1,0:T(8,128)(2,1)}), bf16[256,768]{1,0:T(8,128)(2,1)}) %all-reduce.16.cloned.1.call-update) | async-done | bytes 393232 | tf_op jit(solution)/shard_map/psum | solution.py:230
  462.2 188.9 %while.32 = (s32[]{:T(128)}, f32[256,6,64]{0,2,1:T(8,128)}, f32[8,1024,768]{2,1,0:T(8,128)}, s32[8]{0:T(128)}, bf16[8192,384]{0,1:T(8,128)(2,1)}, /*index=5*/bf1...) while((s32[]{:T(128)}, f32[256,6,64]{0,2,1:T(8,128)}, ...), condition=%wide.region_22.23_spmd.clone, body=%wide.region_21.22_spmd.clone.sunk | while | flops 1023574016 | bytes 87081296 | solution.py:285
  665.1 22.9 %all-reduce.18.cloned.1.call-done = bf16[256,768]{1,0:T(8,128)(2,1)} async-done(((bf16[256,768]{1,0:T(8,128)(2,1)}), bf16[256,768]{1,0:T(8,128)(2,1)}) %all-reduce.18.cloned.1.call-update) | async-done | bytes 393232 | tf_op jit(solution)/shard_map/psum | solution.py:311
  705.2 190.9 %reduce-scatter.2.cloned.1.call-done = f32[128,768]{1,0:T(8,128)} async-done(((f32[8192,768]{1,0:T(8,128)}), f32[128,768]{1,0:T(8,128)}) %reduce-scatter.2.cloned.1.call-update) | async-done | bytes 393232 | tf_op jit(solution)/shard_map/reduce_scatter | solution.py:292
  902.2 318.4 %all-reduce = (f32[2,384]{1,0:T(2,128)}, f32[768]{0:T(1024)}, f32[768]{0:T(1024)}, f32[768]{0:T(1024)}, f32[2,384]{1,0:T(2,128)}, /*index=5*/f32[768]{0:T(1024)}...) all-reduce(f32[2,384]{1,0:T(2,128)S(1)} %pad_maximum_fusion.3, ...), channel_id=1, replica_groups=mesh['dp'=64,'head'=2] {'dp'}, use_global_device_ids=true, to_apply=%region_31.32 | all-reduce | flops 9984 | bytes 79872 | tf_op jit(solution)/shard_map/psum | solution.py:387
  1220.6 371.5 %all-reduce.22.cloned.1.call-done = (f32[3,768,384]{1,2,0:T(8,128)}, f32[384,768]{1,0:T(8,128)}, f32[768,384]{1,0:T(8,128)}, f32[2,768,384]{1,2,0:T(8,128)}, f32...) async-done(((f32[3,768,384]{1,2,0:T(8,128)}, f32[384,768]{1,0:T(8,128)}, f32[768,384]{1,0:T(8,128)}, f32[2,768,384]{1,2,0:T(8,128)}, f32[384,768]{1,0:T(8,128)}, ...) | async-done | bytes 18874384 | tf_op jit(solution)/shard_map/psum | solution.py:387
  1592.1 5.3 copy.113
  (543 shorter events, 374.1 us)
Async XLA Ops:
  8.0 365.4 %copy-start = (bf16[768,1536]{1,0:T(8,128)(2,1)S(1)}, bf16[768,1536]{1,0:T(8,128)(2,1)}, u32[]{:S(2)}) copy-start(bf16[768,1536]{1,0:T(8,128)(2,1)} %param.45) | copy-start | bytes 7077892
  8.0 197.3 %all-reduce.10.cloned.1.call-start = ((), (), s32[]{:S(2)}) async-start(), calls=%async_computation.1 | async-start | bytes 786432 | tf_op jit(solution)/shard_map/psum | solution.py:159
  16.3 194.0 %all-gather.7.cloned.1.call-start = ((), (), s32[]{:S(2)}) async-start(), calls=%async_computation.9 | async-start | bytes 6389760 | tf_op jit(solution)/shard_map/all_gather | solution.py:187
  18.8 191.5 %all-gather.5.cloned.1.call-start = ((), (), s32[]{:S(2)}) async-start(), calls=%async_computation.2 | async-start | bytes 6389760 | tf_op jit(solution)/shard_map/all_gather | solution.py:188
  19.7 351.9 %all-reduce.12.cloned.1.call-start = ((), (), s32[]{:S(2)}) async-start(), calls=%async_computation.3 | async-start | bytes 786432 | tf_op jit(solution)/shard_map/psum | solution.py:197
  99.7 7.0 copy-start.87
  99.7 7.0 copy-start.95
  99.7 105.7 %copy-start.7 = (bf16[256,768]{1,0:T(8,128)(2,1)S(1)}, bf16[256,768]{1,0:T(8,128)(2,1)}, u32[]{:S(2)}) copy-start(bf16[256,768]{1,0:T(8,128)(2,1)} %param.28) | copy-start | bytes 1179652
  106.7 101.3 %copy-start.65 = (f32[768]{0:T(1024)}, f32[768]{0:T(1024)S(1)}, u32[]{:S(2)}) copy-start(f32[768]{0:T(1024)S(1)} %convert_element_type.269) | copy-start | bytes 9220
  106.7 101.2 %copy-start.55 = (f32[768]{0:T(1024)}, f32[768]{0:T(1024)S(1)}, u32[]{:S(2)}) copy-start(f32[768]{0:T(1024)S(1)} %convert_element_type.268) | copy-start | bytes 9220
  106.7 101.2 %copy-start.51 = (f32[768]{0:T(1024)}, f32[768]{0:T(1024)S(1)}, u32[]{:S(2)}) copy-start(f32[768]{0:T(1024)S(1)} %convert_element_type.267) | copy-start | bytes 9220
  345.4 69.3 %all-reduce.14.cloned.1.call-start = ((), (), s32[]{:S(2)}) async-start(), calls=%async_computation.4 | async-start | bytes 786432 | tf_op jit(solution)/shard_map/psum | solution.py:208
  373.2 85.6 %copy-start.5 = (f32[256,768]{1,0:T(8,128)}, f32[256,768]{1,0:T(8,128)S(1)}, u32[]{:S(2)}) copy-start(f32[256,768]{1,0:T(8,128)S(1)} %get-tuple-element.543) | copy-start | bytes 2359300
  381.1 35.4 %copy-start.27 = (bf16[256,768]{1,0:T(8,128)(2,1)S(1)}, bf16[256,768]{1,0:T(8,128)(2,1)}, u32[]{:S(2)}) copy-start(bf16[256,768]{1,0:T(8,128)(2,1)} %param.51) | copy-start | bytes 1179652
  381.2 75.3 %all-reduce.16.cloned.1.call-start = ((), (), s32[]{:S(2)}) async-start(), calls=%async_computation.5 | async-start | bytes 786432 | tf_op jit(solution)/shard_map/psum | solution.py:230
  421.2 35.2 %copy-start.49 = (f32[768]{0:T(1024)S(1)}, f32[768]{0:T(1024)}, u32[]{:S(2)}) copy-start(f32[768]{0:T(1024)} %convert_element_type.281) | copy-start | bytes 9220
  421.2 35.2 %copy-start.58 = (f32[256]{0:T(256)S(1)}, f32[256]{0:T(256)}, u32[]{:S(2)}) copy-start(f32[256]{0:T(256)} %copy-done.57) | copy-start | bytes 3076
  421.2 35.2 %copy-start.63 = (f32[256]{0:T(256)S(1)}, f32[256]{0:T(256)}, u32[]{:S(2)}) copy-start(f32[256]{0:T(256)} %copy-done.62) | copy-start | bytes 3076
  422.8 36.0 %copy-start.16 = (f32[256,768]{1,0:T(8,128)S(1)}, f32[256,768]{1,0:T(8,128)}, u32[]{:S(2)}) copy-start(f32[256,768]{1,0:T(8,128)} %copy-done.15) | copy-start | bytes 2359300
  422.9 265.2 %all-reduce.18.cloned.1.call-start = ((), (), s32[]{:S(2)}) async-start(), calls=%async_computation.6 | async-start | bytes 786432 | tf_op jit(solution)/shard_map/psum | solution.py:311
  654.4 241.7 %reduce-scatter.2.cloned.1.call-start = ((), (), s32[]{:S(2)}) async-start(), calls=%async_computation.8 | async-start | bytes 25559040 | tf_op jit(solution)/shard_map/reduce_scatter | solution.py:292
  655.1 245.1 %all-reduce.20.cloned.1.call-start = ((), (), s32[]{:S(2)}) async-start(), calls=%async_computation.7 | async-start | bytes 786432 | tf_op jit(solution)/shard_map/psum | solution.py:366
  703.8 193.5 %copy-start.40 = (bf16[128,768]{1,0:T(8,128)(2,1)S(1)}, bf16[128,768]{1,0:T(8,128)(2,1)}, u32[]{:S(2)}) copy-start(bf16[128,768]{1,0:T(8,128)(2,1)} %param.29) | copy-start | bytes 589828
  703.8 888.3 %all-reduce.22.cloned.1.call-start = ((), (), s32[]{:S(2)}) async-start(), calls=%async_computation.10 | async-start | bytes 37748736 | tf_op jit(solution)/shard_map/psum | solution.py:387
  (114 other events, 328.1 us)
Sparse Core Ops, SparseCore 0:
  16.4 35.7 all-reduce.9
  345.6 25.9 all-reduce.11
  381.3 33.4 all-reduce.13
  423.0 33.4 all-reduce.15
  654.6 33.4 all-reduce.17
  703.9 33.4 all-reduce.19
  899.9 692.1 all-reduce.21
Sparse Core Ops, SparseCore 1:
  20.6 92.8 all-gather.6
  117.2 87.4 all-gather.4
  660.9 235.1 reduce-scatter.1
where the time goes:
time: 1630 us; the launch traced here: 1620 us
  waiting for transfers between devices  673 us (41%)
  blocking collectives  416 us (26%)
  matrix products  263 us (16%)
  local copies, waits for them, and re-layouts  134 us (8%)
  other arithmetic  108 us (7%)
  between operations  17.4 us (1%)
    psum x1, waiting for transfers between devices, shards(): lax.psum((grad_self_proj, grad_self_bias, grad_self_out, grad_self_out_bi...  372 us
    psum x1, blocking collectives, shards(): lax.psum((grad_self_proj, grad_self_bias, grad_self_out, grad_self_out_bi...  318 us
    reduce_scatter x1, waiting for transfers between devices, shards(): lax.psum_scatter(state_parts, 'dp', scatter_dimension=0, tiled=True)  191 us
    all_gather x1, blocking collectives, shards(): lax.all_gather(keep_low, 'dp', axis=0, tiled=True)  97.9 us
    dot_general x1, matrix products, selection_table(): jnp.einsum('tkh,tkl->thl', high_hot, low_hot, preferred_element_type=jnp....  68 us
    dynamic_update_slice x16, local copies, waits for them, and re-layouts, shards(): lax.scan(scan_step, jnp.zeros((tokens_here, heads_here, HEAD_DIM), jnp.fl...  34 us
    reduce_sum x8, other arithmetic, one_block(): new_sum = running_sum * shrink + jnp.sum(powers, axis=-1)  33.8 us
    psum x1, waiting for transfers between devices, shards(): lax.psum(ffn_back_part.astype(jnp.bfloat16), 'head').astype(jnp.float32)  33.3 us
  transfers between devices with their start and end apart: 10, of which 6 were waited for; matrix products, arithmetic and copies ran while one was open for 8% of the time, Pallas kernels for 0%

commit v1 on v0

v1 whole, which is shorter than its diff:
```python
import functools

import jax
import jax.numpy as jnp
from jax import lax
from jax.experimental import pallas as pl
from jax.experimental.pallas import tpu as pltpu
from jax.sharding import Mesh
from jax.sharding import PartitionSpec as P

HEAD_DIM = 64
masked_score = -1e30
TOK = 256
HEADS = 6
PAIRS = HEADS // 2
WIDTH = 384
MODEL = 768
SHARD = 128
KEEP_ROWS = 16
PER_BLOCK = 8
BLOCK = SHARD * PER_BLOCK
SEL_TOKENS = 16
CHUNK = 32
ROWS = HEADS * TOK
FIRST = 4 * TOK


SMALL_COST = pl.CostEstimate(flops=2**20, bytes_accessed=2**16, transcendentals=0)


def nt(left, right):
    return lax.dot_general(
        left, right, (((1,), (1,)), ((), ())), preferred_element_type=jnp.float32
    )


def mm(left, right):
    return jnp.dot(left, right, preferred_element_type=jnp.float32)


def table_kernel(sel_ref, *refs):
    out_ref, counts = refs[-2:]
    high_count = out_ref.shape[0]
    picks = sel_ref.shape[1]
    to_low = lambda value: value.astype(jnp.float32).astype(jnp.bfloat16)
    high_rows = to_low(lax.broadcasted_iota(jnp.int32, (high_count, picks), 0))
    low_rows = to_low(lax.broadcasted_iota(jnp.int32, (SHARD, picks), 0))
    one, zero = jnp.bfloat16(1), jnp.bfloat16(0)
    for token in range(SEL_TOKENS):
        row = sel_ref[token : token + 1, :]
        high_hot = jnp.where(high_rows == to_low(row >> 7), one, zero)
        low_hot = jnp.where(low_rows == to_low(row & 127), one, zero)
        counts[pl.ds(token * high_count, high_count), :] = nt(high_hot, low_hot)
    for high in range(high_count):
        rows = counts[pl.ds(high, SEL_TOKENS, stride=high_count), :]
        out_ref[high] = jnp.where(rows > 0.5, 1.0, 0.0).astype(jnp.bfloat16)


def selection_table(selection, high_count, first, count, table):
    tokens, picks = selection.shape
    start = first // SEL_TOKENS
    given = [] if table is None else [table]
    return pl.pallas_call(
        table_kernel,
        grid=(count // SEL_TOKENS,),
        in_specs=[pl.BlockSpec((SEL_TOKENS, picks), lambda i: (i + start, 0))]
        + [pl.BlockSpec(memory_space=pl.ANY)] * len(given),
        out_specs=pl.BlockSpec((high_count, SEL_TOKENS, SHARD), lambda i: (0, i + start, 0)),
        out_shape=jax.ShapeDtypeStruct((high_count, tokens, SHARD), jnp.bfloat16),
        scratch_shapes=[pltpu.VMEM((SEL_TOKENS * high_count, SHARD), jnp.float32)],
        input_output_aliases={1: 0} if given else {},
        compiler_params=pltpu.CompilerParams(vmem_limit_bytes=40 * 2**20),
        cost_estimate=SMALL_COST,
    )(selection, *given)


def lane_tile(tile):
    return slice(tile * SHARD, (tile + 1) * SHARD)


def pair_lanes(pair, start=0):
    first = start + pair * 2 * HEAD_DIM
    return slice(first, first + 2 * HEAD_DIM)


def cross_forward_kernel(fresh, slots, rows_ref, *refs):
    tables = refs[:PER_BLOCK]
    given = refs[PER_BLOCK + 1 : -8]
    query_ref = refs[PER_BLOCK]
    (
        memory_out,
        powers_ref,
        max_ref,
        sum_ref,
        out_ref,
        marks_ref,
        scores_ref,
        mask_ref,
    ) = refs[-8:]

    @pl.when(pl.program_id(0) == 0)
    def _():
        if fresh:
            max_ref[...] = jnp.full_like(max_ref, masked_score)
            sum_ref[...] = jnp.zeros_like(sum_ref)
            out_ref[...] = jnp.zeros_like(out_ref)
            marks_ref[...] = jnp.zeros_like(marks_ref)
        else:
            for ref, before in zip((max_ref, sum_ref, out_ref, marks_ref), given):
                ref[...] = before[...]

    for j in range(PER_BLOCK):
        memory_out[pl.ds(j * SHARD, SHARD), :] = rows_ref[j, :SHARD, :]
        keep_row = rows_ref[j, SHARD : SHARD + KEEP_ROWS, :SHARD].astype(jnp.float32)[0:1, :]
        kept = tables[j][0].astype(jnp.float32) * keep_row
        mask_ref[:, lane_tile(j)] = jnp.where(kept > 0.5, 0.0, masked_score)
    block = slots[slots.shape[0] - 1] + pl.program_id(0)
    here_lane = lax.broadcasted_iota(jnp.int32, (CHUNK, SHARD), 1) == block

    def score(pair):
        rows = pl.ds(pair * 2 * TOK, 2 * TOK)
        scores_ref[pair % 2] = nt(query_ref[rows, :], memory_out[:, pair_lanes(pair)])

    def mix(pair):
        rows = pl.ds(pair * 2 * TOK, 2 * TOK)
        out_ref[rows, :] += mm(powers_ref[rows, :], memory_out[:, pair_lanes(pair, WIDTH)])

    score(0)
    for pair in range(PAIRS):
        if pair + 1 < PAIRS:
            score(pair + 1)
        for first in range(0, 2 * TOK, CHUNK):
            rows = pl.ds(pair * 2 * TOK + first, CHUNK)
            narrow = pl.ds(first, CHUNK)
            token = pl.ds(first % TOK, CHUNK)
            top = scores_ref[pair % 2, narrow, lane_tile(0)] + mask_ref[token, lane_tile(0)]
            for j in range(1, PER_BLOCK):
                tile = scores_ref[pair % 2, narrow, lane_tile(j)] + mask_ref[token, lane_tile(j)]
                top = jnp.maximum(top, tile)
            old_max = max_ref[rows, :]
            new_max = jnp.maximum(old_max, jnp.max(top, axis=1, keepdims=True))
            shrink = jnp.exp(old_max - new_max)
            max_ref[rows, :] = new_max
            sum_ref[rows, :] = sum_ref[rows, :] * shrink
            out_ref[rows, :] = out_ref[rows, :] * shrink
            marks_ref[rows, :] = jnp.where(here_lane, new_max, marks_ref[rows, :])
        for first in range(0, 2 * TOK, CHUNK):
            rows = pl.ds(pair * 2 * TOK + first, CHUNK)
            narrow = pl.ds(first, CHUNK)
            token = pl.ds(first % TOK, CHUNK)
            new_max = max_ref[rows, :]
            total = sum_ref[rows, :]
            for j in range(PER_BLOCK):
                tile = scores_ref[pair % 2, narrow, lane_tile(j)] + mask_ref[token, lane_tile(j)]
                powers = jnp.exp(tile - new_max)
                total = total + powers
                powers_ref[rows, lane_tile(j)] = powers.astype(jnp.bfloat16)
            sum_ref[rows, :] = total
        if pair:
            mix(pair - 1)
    mix(PAIRS - 1)


def whole(*shape):
    return pl.BlockSpec(shape, lambda *_: (0,) * len(shape))


def cross_forward(slots, rows, table, queries, running):
    shard_count = rows.shape[0]
    blocks = shard_count // PER_BLOCK
    states = shard_count * SHARD
    table_spec = lambda j: pl.BlockSpec(
        (1, TOK, SHARD), lambda i, g: (g[PER_BLOCK * i + j], 0, 0)
    )
    stat = jax.ShapeDtypeStruct((ROWS, SHARD), jnp.float32)
    return pl.pallas_call(
        functools.partial(cross_forward_kernel, not running),
        grid_spec=pltpu.PrefetchScalarGridSpec(
            num_scalar_prefetch=1,
            grid=(blocks,),
            in_specs=[
                pl.BlockSpec((PER_BLOCK, SHARD + KEEP_ROWS, MODEL), lambda i, g: (i, 0, 0)),
                *[table_spec(j) for j in range(PER_BLOCK)],
                whole(ROWS, 2 * HEAD_DIM),
                *[whole(ROWS, SHARD)] * len(running),
            ],
            out_specs=[
                pl.BlockSpec((BLOCK, 2 * WIDTH), lambda i, g: (i, 0)),
                pl.BlockSpec((ROWS, BLOCK), lambda i, g: (0, i)),
                *[whole(ROWS, SHARD)] * 4,
            ],
            scratch_shapes=[
                pltpu.VMEM((2, 2 * TOK, BLOCK), jnp.float32),
                pltpu.VMEM((TOK, BLOCK), jnp.float32),
            ],
        ),
        out_shape=[
            jax.ShapeDtypeStruct((states, 2 * WIDTH), jnp.bfloat16),
            jax.ShapeDtypeStruct((ROWS, states), jnp.bfloat16),
            stat,
            stat,
            stat,
            stat,
        ],
        compiler_params=pltpu.CompilerParams(vmem_limit_bytes=56 * 2**20),
        cost_estimate=SMALL_COST,
    )(slots, rows, *([table] * PER_BLOCK), queries, *running)


def cross_backward_kernel(
    fresh,
    base_ref,
    memory_ref,
    powers_ref,
    scale_ref,
    scale_rows_ref,
    upstream_ref,
    turned_query_ref,
    turned_upstream_ref,
    delta_ref,
    *refs,
):
    query_out, bias_out, state_out, grad_ref, change_ref, spread_ref = refs[-6:]

    @pl.when(pl.program_id(0) == 0)
    def _():
        if fresh:
            query_out[...] = jnp.zeros_like(query_out)
            bias_out[...] = jnp.zeros_like(bias_out)
        else:
            query_out[...] = refs[0][...]
            bias_out[...] = refs[1][...]

    block = base_ref[0] + pl.program_id(0)
    here_lane = lax.broadcasted_iota(jnp.int32, (CHUNK, SHARD), 1) == block
    key_start = base_ref[1] * WIDTH
    value_start = (1 - base_ref[1]) * WIDTH
    spots = [
        pl.multiple_of(base_ref[2 + pl.program_id(0) * PER_BLOCK + j] * SHARD, SHARD)
        for j in range(PER_BLOCK)
    ]

    def put(start, grad):
        rows = pl.ds(pl.multiple_of(start, HEAD_DIM), HEAD_DIM)
        for j in range(PER_BLOCK):
            state_out[rows, pl.ds(spots[j], SHARD)] = grad[:, lane_tile(j)].astype(jnp.bfloat16)

    def spread(pair):
        rows = pl.ds(pair * 2 * TOK, 2 * TOK)
        grad_ref[pair % 2] = nt(upstream_ref[rows, :], memory_ref[:, pair_lanes(pair, WIDTH)])

    def finish(pair):
        rows = pl.ds(pair * 2 * TOK, 2 * TOK)
        query_out[rows, :] += mm(change_ref[pair % 2], memory_ref[:, pair_lanes(pair)])
        for side in range(2):
            head = 2 * pair + side
            change = change_ref[pair % 2, side * TOK : (side + 1) * TOK, :]
            key_grad = mm(turned_query_ref[pl.ds(head * HEAD_DIM, HEAD_DIM), :], change)
            put(key_start + head * HEAD_DIM, key_grad)

    spread(0)
    for first in range(0, ROWS, CHUNK):
        rows = pl.ds(first, CHUNK)
        scale = jnp.sum(jnp.where(here_lane, scale_ref[rows, :], 0.0), axis=1, keepdims=True)
        spread_ref[rows, :] = jnp.broadcast_to(scale, (CHUNK, SHARD))
    for pair in range(PAIRS):
        if pair + 1 < PAIRS:
            spread(pair + 1)
        for first in range(0, 2 * TOK, CHUNK):
            rows = pl.ds(pair * 2 * TOK + first, CHUNK)
            narrow = pl.ds(first, CHUNK)
            scale = spread_ref[rows, :]
            delta = delta_ref[rows, :]
            for j in range(PER_BLOCK):
                powers = powers_ref[rows, lane_tile(j)].astype(jnp.float32)
                change = powers * ((grad_ref[pair % 2, narrow, lane_tile(j)] - delta) * scale)
                change_ref[pair % 2, narrow, lane_tile(j)] = change.astype(jnp.bfloat16)
        for head in (2 * pair, 2 * pair + 1):
            narrow = pl.ds(head * HEAD_DIM, HEAD_DIM)
            scaled = turned_upstream_ref[narrow, :] * scale_rows_ref[0, head : head + 1, :]
            value_grad = mm(scaled.astype(jnp.bfloat16), powers_ref[pl.ds(head * TOK, TOK), :])
            put(value_start + head * HEAD_DIM, value_grad)
            total = bias_out[narrow, :]
            for j in range(PER_BLOCK):
                total = total + value_grad[:, lane_tile(j)]
            bias_out[narrow, :] = total
        if pair:
            finish(pair - 1)
    finish(PAIRS - 1)


def cross_backward(base, memory, powers, operands, running):
    states = memory.shape[0]
    blocks = states // BLOCK
    return pl.pallas_call(
        functools.partial(cross_backward_kernel, not running),
        grid_spec=pltpu.PrefetchScalarGridSpec(
            num_scalar_prefetch=1,
            grid=(blocks,),
            in_specs=[
                pl.BlockSpec((BLOCK, 2 * WIDTH), lambda i, b: (i, 0)),
                pl.BlockSpec((ROWS, BLOCK), lambda i, b: (0, i)),
                whole(ROWS, SHARD),
                pl.BlockSpec((1, 8, TOK), lambda i, b: (b[0] + i, 0, 0)),
                whole(ROWS, 2 * HEAD_DIM),
                whole(WIDTH, TOK),
                whole(WIDTH, TOK),
                whole(ROWS, SHARD),
                *[whole(ROWS, SHARD), whole(WIDTH, SHARD)][: len(running)],
            ],
            out_specs=[
                whole(ROWS, SHARD),
                whole(WIDTH, SHARD),
                whole(2 * WIDTH, states),
            ],
            scratch_shapes=[
                pltpu.VMEM((2, 2 * TOK, BLOCK), jnp.float32),
                pltpu.VMEM((2, 2 * TOK, BLOCK), jnp.bfloat16),
                pltpu.VMEM((ROWS, SHARD), jnp.float32),
            ],
        ),
        out_shape=[
            jax.ShapeDtypeStruct((ROWS, SHARD), jnp.float32),
            jax.ShapeDtypeStruct((WIDTH, SHARD), jnp.float32),
            jax.ShapeDtypeStruct((2 * WIDTH, states), jnp.bfloat16),
        ],
        compiler_params=pltpu.CompilerParams(vmem_limit_bytes=56 * 2**20),
        cost_estimate=SMALL_COST,
    )(base, memory, powers, *operands, *running)


epsilon = 1e-05
SCALE = HEAD_DIM ** (-0.5)
LANES2 = 2 * HEAD_DIM


def f32(value):
    return value.astype(jnp.float32)


def low16(value):
    return value.astype(jnp.bfloat16)


def left_side(rows):
    return lax.broadcasted_iota(jnp.int32, (rows, LANES2), 1) < HEAD_DIM


def one_side(pair_rows, head):
    left = left_side(pair_rows.shape[0])
    return jnp.where(left if head % 2 == 0 else ~left, pair_rows, 0.0)


def norm_rows(rows, gain, bias):
    centered = rows - jnp.mean(rows, axis=-1, keepdims=True)
    variance = jnp.mean(centered * centered, axis=-1, keepdims=True)
    inverse = lax.rsqrt(variance + epsilon)
    normed = centered * inverse
    return normed * gain + bias, normed, inverse


def norm_rows_back(upstream, normed, inverse, gain):
    scaled = upstream * gain
    mean_one = jnp.mean(scaled, axis=-1, keepdims=True)
    mean_two = jnp.mean(scaled * normed, axis=-1, keepdims=True)
    return inverse * (scaled - mean_one - normed * mean_two)


def column_sum(rows):
    return jnp.sum(rows, axis=0, keepdims=True)


def gelu_parts(values):
    inner = 0.5 * (1.0 + lax.erf(values * (0.5**0.5)))
    return inner


def dense_call(kernel, outs, *operands):
    shapes = [jax.ShapeDtypeStruct(shape, dtype) for shape, dtype in outs]
    return pl.pallas_call(
        kernel,
        in_specs=[pl.BlockSpec(memory_space=pltpu.VMEM)] * len(operands),
        out_specs=[pl.BlockSpec(memory_space=pltpu.VMEM)] * len(outs),
        out_shape=shapes,
        compiler_params=pltpu.CompilerParams(vmem_limit_bytes=56 * 2**20),
        cost_estimate=SMALL_COST,
    )(*operands)


F = jnp.float32
B = jnp.bfloat16


def self_forward_kernel(x_ref, proj_ref, bias_ref, out_ref, q_ref, k_ref, v_ref, attn_ref, mixed_ref, part_ref):
    x = x_ref[...]
    queries = low16(mm(x, proj_ref[0]) + f32(bias_ref[...])[0:1])
    q_ref[...] = low16(f32(queries) * SCALE)
    k_ref[...] = low16(mm(x, proj_ref[1]))
    v_ref[...] = low16(mm(x, proj_ref[2]) + f32(bias_ref[...])[1:2])
    causal = lax.broadcasted_iota(jnp.int32, (TOK, TOK), 0) >= lax.broadcasted_iota(
        jnp.int32, (TOK, TOK), 1
    )
    left = left_side(TOK)
    for pair in range(PAIRS):
        lanes = pair_lanes(pair)
        mixes = []
        for head in (2 * pair, 2 * pair + 1):
            query = low16(one_side(f32(q_ref[:, lanes]), head))
            scores = jnp.where(causal, nt(query, k_ref[:, lanes]), masked_score)
            powers = jnp.exp(scores - jnp.max(scores, axis=1, keepdims=True))
            attn = powers / jnp.sum(powers, axis=1, keepdims=True)
            attn_ref[head] = attn
            mixes.append(mm(low16(attn), v_ref[:, lanes]))
        mixed_ref[:, lanes] = low16(jnp.where(left, mixes[0], mixes[1]))
    part_ref[...] = low16(mm(mixed_ref[...], out_ref[...]))


def self_forward(x, proj, bias, out_weight):
    return dense_call(
        self_forward_kernel,
        [((TOK, WIDTH), B)] * 3
        + [((HEADS, TOK, TOK), F), ((TOK, WIDTH), B), ((TOK, MODEL), B)],
        x,
        proj,
        bias,
        out_weight,
    )


def first_norm_kernel(x_ref, part_ref, got_ref, rows_ref, weight_ref, bias_ref, after_ref, normed_ref, inverse_ref, low_ref, stack_ref, turned_ref):
    total = f32(x_ref[...]) + (f32(part_ref[...]) + f32(got_ref[...])) + rows_ref[0:1]
    after, normed, inverse = norm_rows(total, rows_ref[1:2], rows_ref[2:3])
    after_ref[...] = after
    normed_ref[...] = normed
    inverse_ref[...] = jnp.broadcast_to(inverse, (TOK, SHARD))
    low_ref[...] = low16(after)
    queries = f32(low16(mm(low_ref[...], weight_ref[...]) + bias_ref[...])) * SCALE
    for head in range(HEADS):
        lanes = pair_lanes(head // 2)
        stack_ref[pl.ds(head * TOK, TOK), :] = low16(one_side(queries[:, lanes], head))
    turned_ref[...] = low16(jnp.transpose(queries))


def first_norm(x, part, got, rows, weight, bias):
    return dense_call(
        first_norm_kernel,
        [
            ((TOK, MODEL), F),
            ((TOK, MODEL), F),
            ((TOK, SHARD), F),
            ((TOK, MODEL), B),
            ((ROWS, LANES2), B),
            ((WIDTH, TOK), B),
        ],
        x,
        part,
        got,
        rows,
        weight,
        bias,
    )


def recall_kernel(mixed_ref, max_ref, sum_ref, marks_ref, weight_ref, full_ref, low_ref, scale_ref, scale_rows_ref, part_ref):
    left = left_side(TOK)
    used = lax.broadcasted_iota(jnp.int32, (TOK, SHARD), 1) < scale_rows_ref.shape[0]
    scale_rows_ref[...] = jnp.zeros_like(scale_rows_ref)
    for pair in range(PAIRS):
        sides = []
        for head in (2 * pair, 2 * pair + 1):
            rows = pl.ds(head * TOK, TOK)
            inverse = 1.0 / jnp.sum(sum_ref[rows, :], axis=1, keepdims=True)
            sides.append(mixed_ref[rows, :] * inverse)
            scales = jnp.where(used, jnp.exp(marks_ref[rows, :] - max_ref[rows, :]) * inverse, 0.0)
            scale_ref[rows, :] = scales
            scale_rows_ref[:, head, :] = jnp.transpose(scales)[: scale_rows_ref.shape[0], :]
        recalled = jnp.where(left, sides[0], sides[1])
        full_ref[:, pair_lanes(pair)] = recalled
        low_ref[:, pair_lanes(pair)] = low16(recalled)
    part_ref[...] = low16(mm(low_ref[...], weight_ref[...]))


def recall(mixed, top, total, marks, weight, blocks):
    return dense_call(
        recall_kernel,
        [
            ((TOK, WIDTH), F),
            ((TOK, WIDTH), B),
            ((ROWS, SHARD), F),
            ((blocks, 8, TOK), F),
            ((TOK, MODEL), B),
        ],
        mixed,
        top,
        total,
        marks,
        weight,
    )


def expand_kernel(after_ref, part_ref, got_ref, rows_ref, expand_ref, bias_ref, reduce_ref, cross_ref, normed_ref, inverse_ref, low_ref, units_ref, hidden_ref, out_ref):
    total = after_ref[...] + (f32(part_ref[...]) + f32(got_ref[...])) + rows_ref[0:1]
    after, normed, inverse = norm_rows(total, rows_ref[1:2], rows_ref[2:3])
    cross_ref[...] = after
    normed_ref[...] = normed
    inverse_ref[...] = jnp.broadcast_to(inverse, (TOK, SHARD))
    low_ref[...] = low16(after)
    units = mm(low_ref[...], expand_ref[...]) + bias_ref[...]
    units_ref[...] = units
    hidden_ref[...] = low16(units * gelu_parts(units))
    out_ref[...] = low16(mm(hidden_ref[...], reduce_ref[...]))


def expand(after, part, got, rows, expand_weight, bias, reduce_weight):
    units = expand_weight.shape[1]
    return dense_call(
        expand_kernel,
        [
            ((TOK, MODEL), F),
            ((TOK, MODEL), F),
            ((TOK, SHARD), F),
            ((TOK, MODEL), B),
            ((TOK, units), F),
            ((TOK, units), B),
            ((TOK, MODEL), B),
        ],
        after,
        part,
        got,
        rows,
        expand_weight,
        bias,
        reduce_weight,
    )


def expand_back_kernel(cross_ref, part_ref, got_ref, rows_ref, upstream_ref, units_ref, expand_ref, reduce_ref, layer_ref, grad_ref, grad_low_ref, units_low_ref, out_ref, sums_ref, unit_sums_ref):
    total = cross_ref[...] + (f32(part_ref[...]) + f32(got_ref[...])) + rows_ref[0:1]
    after, normed, inverse = norm_rows(total, rows_ref[1:2], rows_ref[2:3])
    layer_ref[...] = low16(after)
    upstream = f32(upstream_ref[...])
    grad = norm_rows_back(upstream, normed, inverse, rows_ref[1:2])
    grad_ref[...] = grad
    grad_low_ref[...] = low16(grad)
    sums_ref[...] = jnp.zeros_like(sums_ref)
    sums_ref[0:1, :] = column_sum(grad)
    sums_ref[1:2, :] = column_sum(upstream * normed)
    sums_ref[2:3, :] = column_sum(upstream)
    grad_hidden = f32(low16(nt(grad_low_ref[...], reduce_ref[...])))
    units = units_ref[...]
    density = jnp.exp(-0.5 * units * units) * (0.5 / jnp.pi) ** 0.5
    grad_units = grad_hidden * (gelu_parts(units) + units * density)
    unit_sums_ref[...] = jnp.zeros_like(unit_sums_ref)
    unit_sums_ref[0:1, :] = column_sum(grad_units)
    units_low_ref[...] = low16(grad_units)
    out_ref[...] = low16(nt(units_low_ref[...], expand_ref[...]))


def expand_back(cross, part, got, rows, upstream, units, expand_weight, reduce_weight):
    count = expand_weight.shape[1]
    return dense_call(
        expand_back_kernel,
        [
            ((TOK, MODEL), B),
            ((TOK, MODEL), F),
            ((TOK, MODEL), B),
            ((TOK, count), B),
            ((TOK, MODEL), B),
            ((8, MODEL), F),
            ((8, count), F),
        ],
        cross,
        part,
        got,
        rows,
        upstream,
        units,
        expand_weight,
        reduce_weight,
    )


def second_back_kernel(grad_ref, part_ref, got_ref, rows_ref, normed_ref, inverse_ref, weight_ref, full_ref, max_ref, out_ref, low_ref, sums_ref, stack_ref, turned_ref, delta_ref):
    upstream = grad_ref[...] + (f32(part_ref[...]) + f32(got_ref[...]))
    normed = normed_ref[...]
    grad = norm_rows_back(upstream, normed, inverse_ref[:, 0:1], rows_ref[1:2])
    out_ref[...] = grad
    low_ref[...] = low16(grad)
    sums_ref[...] = jnp.zeros_like(sums_ref)
    sums_ref[0:1, :] = column_sum(grad)
    sums_ref[1:2, :] = column_sum(upstream * normed)
    sums_ref[2:3, :] = column_sum(upstream)
    recalled_grad = f32(low16(nt(low_ref[...], weight_ref[...])))
    turned_ref[...] = jnp.transpose(recalled_grad)
    for head in range(HEADS):
        rows = pl.ds(head * TOK, TOK)
        lanes = pair_lanes(head // 2)
        flags = max_ref[rows, :] > 0.1 * masked_score
        own = one_side(recalled_grad[:, lanes], head)
        delta = jnp.sum(own * full_ref[:, lanes], axis=1, keepdims=True)
        delta_ref[rows, :] = jnp.where(flags, jnp.broadcast_to(delta, (TOK, SHARD)), 0.0)
        stack_ref[rows, :] = low16(jnp.where(flags, own, 0.0))


def second_back(grad, part, got, rows, normed, inverse, weight, full, top):
    return dense_call(
        second_back_kernel,
        [
            ((TOK, MODEL), F),
            ((TOK, MODEL), B),
            ((8, MODEL), F),
            ((ROWS, LANES2), B),
            ((WIDTH, TOK), F),
            ((ROWS, SHARD), F),
        ],
        grad,
        part,
        got,
        rows,
        normed,
        inverse,
        weight,
        full,
        top,
    )


def query_back_kernel(grad_ref, weight_ref, low_ref, part_ref, sums_ref):
    left = left_side(TOK)
    for pair in range(PAIRS):
        first = grad_ref[pl.ds(2 * pair * TOK, TOK), :]
        second = grad_ref[pl.ds((2 * pair + 1) * TOK, TOK), :]
        low_ref[:, pair_lanes(pair)] = low16(jnp.where(left, first, second) * SCALE)
    sums_ref[...] = jnp.zeros_like(sums_ref)
    sums_ref[0:1, :] = column_sum(f32(low_ref[...]))
    part_ref[...] = low16(nt(low_ref[...], weight_ref[...]))


def query_back(grad, weight):
    return dense_call(
        query_back_kernel,
        [((TOK, WIDTH), B), ((TOK, MODEL), B), ((8, WIDTH), F)],
        grad,
        weight,
    )


def self_back_kernel(grad_ref, part_ref, got_ref, rows_ref, normed_ref, inverse_ref, out_weight_ref, q_ref, k_ref, v_ref, attn_ref, proj_ref, out_ref, low_ref, sums_ref, dq_ref, dk_ref, dv_ref, back_ref, bias_ref):
    upstream = grad_ref[...] + (f32(part_ref[...]) + f32(got_ref[...]))
    normed = normed_ref[...]
    grad = norm_rows_back(upstream, normed, inverse_ref[:, 0:1], rows_ref[1:2])
    out_ref[...] = grad
    low_ref[...] = low16(grad)
    sums_ref[...] = jnp.zeros_like(sums_ref)
    sums_ref[0:1, :] = column_sum(grad)
    sums_ref[1:2, :] = column_sum(upstream * normed)
    sums_ref[2:3, :] = column_sum(upstream)
    mixed = low16(nt(low_ref[...], out_weight_ref[...]))
    left = left_side(TOK)
    for pair in range(PAIRS):
        lanes = pair_lanes(pair)
        mixed_pair = mixed[:, lanes]
        query_parts, key_parts, value_parts = [], [], []
        for head in (2 * pair, 2 * pair + 1):
            attn = attn_ref[head]
            grad_attn = nt(low16(one_side(f32(mixed_pair), head)), v_ref[:, lanes])
            center = jnp.sum(attn * grad_attn, axis=1, keepdims=True)
            change = attn * (grad_attn - center)
            change_low = low16(change)
            query_parts.append(mm(change_low, k_ref[:, lanes]))
            key_parts.append(mm(low16(jnp.transpose(f32(change_low))), q_ref[:, lanes]))
            value_parts.append(mm(low16(jnp.transpose(attn)), mixed_pair))
        dq_ref[:, lanes] = low16(jnp.where(left, query_parts[0], query_parts[1]) * SCALE)
        dk_ref[:, lanes] = low16(jnp.where(left, key_parts[0], key_parts[1]))
        dv_ref[:, lanes] = low16(jnp.where(left, value_parts[0], value_parts[1]))
    back = nt(dq_ref[...], proj_ref[0]) + nt(dk_ref[...], proj_ref[1]) + nt(dv_ref[...], proj_ref[2])
    back_ref[...] = low16(back)
    bias_ref[...] = jnp.zeros_like(bias_ref)
    bias_ref[0:1, :] = column_sum(f32(dq_ref[...]))
    bias_ref[1:2, :] = column_sum(f32(dv_ref[...]))


def self_back(grad, part, got, rows, normed, inverse, out_weight, queries, keys, values, attn, proj):
    return dense_call(
        self_back_kernel,
        [
            ((TOK, MODEL), F),
            ((TOK, MODEL), B),
            ((8, MODEL), F),
            ((TOK, WIDTH), B),
            ((TOK, WIDTH), B),
            ((TOK, WIDTH), B),
            ((TOK, MODEL), B),
            ((8, WIDTH), F),
        ],
        grad,
        part,
        got,
        rows,
        normed,
        inverse,
        out_weight,
        queries,
        keys,
        values,
        attn,
        proj,
    )


def finish_kernel(core_ref, mine0_ref, other0_ref, mine1_ref, other1_ref, memory_ref, query_ref, out_ref, proj_ref, self_ref, turned_ref):
    even = core_ref[0] == 0
    rows = MODEL // 32
    for y in range(2):
        for z in range(2):
            for x in range(4):
                at = pl.ds(((y * 2 + z) * 4 + x) * rows, rows)
                first = jnp.where(even, mine0_ref[x, y, z], other0_ref[x, y, z]).astype(F)
                second = jnp.where(even, other1_ref[y, x, z], mine1_ref[y, x, z]).astype(F)
                memory_ref[0, at, :] = first[:rows, :WIDTH]
                query_ref[at, :] = first[:rows, WIDTH:]
                proj_ref[0, at, :] = first[rows : 2 * rows, :WIDTH]
                proj_ref[1, at, :] = first[rows : 2 * rows, WIDTH:]
                memory_ref[1, at, :] = second[:rows, :WIDTH]
                turned_ref[0, at, :] = second[:rows, WIDTH:]
                proj_ref[2, at, :] = second[rows : 2 * rows, :WIDTH]
                turned_ref[1, at, :] = second[rows : 2 * rows, WIDTH:]
    out_ref[...] = jnp.transpose(turned_ref[0])
    self_ref[...] = jnp.transpose(turned_ref[1])


def finish(core, mine, other):
    rows = mine.shape[3]
    first = pl.BlockSpec((4, 2, 2, rows, MODEL), lambda i, c: (0, i, 0, 0, 0))
    second = pl.BlockSpec((2, 4, 2, rows, MODEL), lambda i, c: (i, 0, 0, 0, 0))
    half = MODEL // 2
    return pl.pallas_call(
        finish_kernel,
        grid_spec=pltpu.PrefetchScalarGridSpec(
            num_scalar_prefetch=1,
            grid=(2,),
            in_specs=[first, first, second, second],
            out_specs=[
                pl.BlockSpec((2, half, WIDTH), lambda i, c: (0, i, 0)),
                pl.BlockSpec((half, WIDTH), lambda i, c: (i, 0)),
                pl.BlockSpec((WIDTH, half), lambda i, c: (0, i)),
                pl.BlockSpec((3, half, WIDTH), lambda i, c: (0, i, 0)),
                pl.BlockSpec((WIDTH, half), lambda i, c: (0, i)),
            ],
            scratch_shapes=[pltpu.VMEM((2, half, WIDTH), F)],
        ),
        out_shape=[
            jax.ShapeDtypeStruct((2, MODEL, WIDTH), F),
            jax.ShapeDtypeStruct((MODEL, WIDTH), F),
            jax.ShapeDtypeStruct((WIDTH, MODEL), F),
            jax.ShapeDtypeStruct((3, MODEL, WIDTH), F),
            jax.ShapeDtypeStruct((WIDTH, MODEL), F),
        ],
        compiler_params=pltpu.CompilerParams(vmem_limit_bytes=56 * 2**20),
        cost_estimate=SMALL_COST,
    )(core, mine, other, mine, other)


RING = 4


def place(y, z, x, core):
    return (((y % RING) * 2 + z % 2) * RING + x % RING) * 2 + core % 2


def every_place():
    return [
        (y, z, x, core)
        for y in range(RING)
        for z in range(2)
        for x in range(RING)
        for core in range(2)
    ]


def here():
    return tuple(lax.axis_index(name) for name in DP)


DP = ("y", "z", "x", "core")


def partner(level, y, z, x, core):
    if level == "core":
        return y, z, x, 1 - core
    if level == "depth":
        return y, 1 - z, x, core
    flip = 1 if level[1] == "1" else 3
    if (level[0] == "a") == (core == 0):
        return y, z, x ^ flip, core
    return y ^ flip, z, x, core


def exchange(array, level):
    pairs = [(place(*at), place(*partner(level, *at))) for at in every_place()]
    return lax.ppermute(array, DP, pairs)


def swap_depth(array):
    pairs = []
    for y, z, x, core in every_place():
        for head in range(2):
            pairs.append(
                (place(y, z, x, core) * 2 + head, place(y, z + 1, x, core) * 2 + 1 - head)
            )
    return lax.ppermute(array, DP + ("head",), pairs)


def project(states, keep_rows, weights, bias_row):
    memory = jnp.dot(states, weights, preferred_element_type=jnp.float32) + bias_row
    return jnp.concatenate([memory.astype(jnp.bfloat16), keep_rows], axis=0)


def gather_plane(shard):
    return lax.all_gather(shard, ("y", "x"), axis=0, tiled=True)


def core_slots(depth, side):
    return jnp.stack([place(a, depth, b, side) for a in range(RING) for b in range(RING)])


def far_slots(depth, side):
    y, z, x, core = here()
    steps = [(a, b) for a in range(RING) for b in range(RING)]
    first = jnp.stack([place(y + b, depth, x + a, 0) for a, b in steps])
    second = jnp.stack([place(y + a, depth, x + b, 1) for a, b in steps])
    return jnp.where(side == 0, first, second)


def rounded(rows):
    return lax.reduce_precision(rows, 8, 7)


def two_terms(rows):
    high = rounded(rows)
    low = rounded(rows - high)
    return jnp.concatenate([high, low], axis=0).astype(jnp.bfloat16)


def one_term(rows):
    count = rows.shape[0] // 2
    return rows[:count].astype(jnp.float32) + rows[count:].astype(jnp.float32)


CHIPS = ("y", "z", "x")
CHIP_COUNT = RING * RING * 2
EXTRA_ROWS = 8


def reduce_chips(totals, extra):
    lanes = totals[0].shape[1]
    chunks = [total.astype(jnp.bfloat16).reshape(CHIP_COUNT, -1, lanes) for total in totals]
    if extra is not None:
        terms = two_terms(extra.reshape(CHIP_COUNT, -1)).reshape(2, CHIP_COUNT, -1)
        terms = jnp.concatenate([terms[0], terms[1]], axis=1)[:, None, :]
        filler = jnp.zeros((CHIP_COUNT, EXTRA_ROWS - 1, lanes), jnp.bfloat16)
        chunks += [terms, filler]
    return lax.all_to_all(jnp.concatenate(chunks, axis=1), CHIPS, 0, 0, tiled=True)


def chip_sum(chunks):
    return jnp.sum(chunks.astype(jnp.float32), axis=0)


def move_axis(array, which, step):
    pairs = []
    for y, z, x, core in every_place():
        if (which == "a") == (core == 0):
            to = place(y, z, x + step, core)
        else:
            to = place(y + step, z, x, core)
        pairs.append((place(y, z, x, core), to))
    return lax.ppermute(array, DP, pairs)


def spread_ring(piece, which):
    y, z, x, core = here()
    spot = jnp.where((core == 0) == (which == "a"), x, y)
    got = [piece] + [move_axis(piece, which, -step) for step in (1, 2, 3)]
    ordered = []
    for chunk in range(RING):
        step = (chunk - spot) % RING
        near = jnp.where(step == 0, got[0], got[1])
        ordered.append(jnp.where(step < 2, near, jnp.where(step == 2, got[2], got[3])))
    return jnp.stack(ordered)


def spread_depth(piece):
    z = lax.axis_index("z")
    other = exchange(piece, "depth")
    return jnp.where(z == 0, jnp.stack([piece, other]), jnp.stack([other, piece]))


def by_core(mine, even):
    other = exchange(mine, "core")
    return jnp.where(even, mine, other), jnp.where(even, other, mine)


def turned_dot(left, right):
    return jnp.einsum("sd,se->de", left, right, preferred_element_type=jnp.float32)


def own_and_sent(even, left, right, other_left, other_right):
    mine = turned_dot(jnp.where(even, left, other_left), jnp.where(even, right, other_right))
    sent = turned_dot(jnp.where(even, other_left, left), jnp.where(even, other_right, right))
    return mine, sent.astype(jnp.bfloat16)


def swap_heads(part):
    return lax.ppermute(part, "head", [(0, 1), (1, 0)])


def three_rows(*rows):
    rows = [row.astype(jnp.float32)[None] for row in rows]
    return jnp.concatenate(rows + [jnp.zeros((8 - len(rows), rows[0].shape[1]))], axis=0)


def shards(
    decoder_in,
    encoder_states,
    keep_mask,
    selection,
    self_proj,
    self_bias,
    self_out,
    self_out_bias,
    norm1_gain,
    norm1_bias,
    cross_query,
    cross_memory,
    cross_bias,
    cross_out,
    cross_out_bias,
    norm2_gain,
    norm2_bias,
    expand_weight,
    expand_bias,
    reduce_weight,
    reduce_bias,
    norm3_gain,
    norm3_bias,
    out_cotangent,
):
    even = lax.axis_index("core") == 0
    core = lax.axis_index("core")
    depth = lax.axis_index("z")
    barrier = lax.optimization_barrier
    tie = lambda value, other: barrier((value, other))[0]

    cross_rows = cross_bias.astype(jnp.float32)
    bias_row = jnp.concatenate([jnp.zeros((1, WIDTH), jnp.float32), cross_rows[1:2]], axis=1)
    memory_weights = jnp.concatenate([cross_memory[0], cross_memory[1]], axis=1)
    keep_rows = jnp.zeros((KEEP_ROWS, MODEL), jnp.bfloat16)
    keep_rows = keep_rows.at[0, :SHARD].set(keep_mask.astype(jnp.bfloat16))
    far = swap_depth(jnp.concatenate([encoder_states, keep_rows], axis=0))
    near_rows = gather_plane(project(encoder_states, keep_rows, memory_weights, bias_row))

    queries, keys, values, attn, mixed_low, part = self_forward(
        decoder_in, self_proj, self_bias, self_out
    )
    got = swap_heads(part)
    far, selection = barrier((far, selection, part))[:2]
    far_states = far[:SHARD]
    far_rows = project(far_states, far[SHARD:], memory_weights, bias_row)
    far_row = [far_rows] + [move_axis(far_rows, "b", -step) for step in (1, 2, 3)]
    table = selection_table(selection, 64, 0, TOK, None)
    got, far_row, table = barrier((got, far_row, table))
    far_row = jnp.concatenate(far_row, axis=0)
    far_rows = [far_row] + [move_axis(far_row, "a", -step) for step in (1, 2, 3)]
    norm1_rows = three_rows(self_out_bias, norm1_gain, norm1_bias)
    after_self, normed1, inverse1, after_self_low, query_stack, turned_queries = first_norm(
        decoder_in, part, got, norm1_rows, cross_query, cross_rows[0:1]
    )

    running = ()
    kept = []
    block = 0
    near_rows, table = barrier((near_rows, table))
    for at in (depth, 1 - depth):
        if block:
            far_rows = barrier((far_rows, near_stats))[0]
            mine, order = jnp.concatenate(far_rows, axis=0), far_slots
        else:
            mine, order = near_rows, core_slots
        for side, rows in ((core, mine), (1 - core, exchange(mine, "core"))):
            slots = order(at, side)
            bases = jnp.concatenate([slots, jnp.full((1,), block, slots.dtype)])
            memory, powers, *running = cross_forward(
                bases,
                rows.reshape(slots.shape[0], SHARD + KEEP_ROWS, MODEL),
                table,
                query_stack,
                running,
            )
            spots = ((slots // 16) * RING + (slots // 2) % RING).astype(jnp.int32)
            kept.append((block, spots, memory, powers))
            if block == 0:
                near_stats = running[1][:1]
                near_states, far_states, _ = barrier((encoder_states, far_states, near_stats))
                near_states = gather_plane(near_states)
                far_states = gather_plane(far_states)
            block += slots.shape[0] // PER_BLOCK
    top, total, mixed, marks = running
    recalled_full, recalled, scales, scale_rows, part = recall(
        mixed, top, total, marks, cross_out, block
    )
    norm2_rows = three_rows(cross_out_bias, norm2_gain, norm2_bias)
    after_cross, normed2, inverse2, after_cross_low, units, hidden, part = expand(
        after_self,
        part,
        swap_heads(part),
        norm2_rows,
        expand_weight,
        expand_bias.astype(jnp.float32)[None],
        reduce_weight,
    )
    norm3_rows = three_rows(reduce_bias, norm3_gain, norm3_bias)
    layer_out, grad_r3, grad_r3_low, units_low, part, sums3, unit_sums = expand_back(
        after_cross,
        part,
        swap_heads(part),
        norm3_rows,
        out_cotangent,
        units,
        expand_weight,
        reduce_weight,
    )
    got = swap_heads(part)

    half_units = units_low.shape[1] // 2
    wide_keep, wide_sent = [], []
    for lanes in (slice(0, half_units), slice(half_units, 2 * half_units)):
        mine, sent = own_and_sent(
            even, hidden[:, lanes], grad_r3_low, after_cross_low, units_low[:, lanes]
        )
        wide_keep.append(mine)
        wide_sent.append(sent)
    wide = jnp.concatenate(wide_keep, axis=0) + exchange(
        jnp.concatenate(wide_sent, axis=0), "core"
    ).astype(jnp.float32)
    wide = wide.astype(jnp.bfloat16)

    grad_r2, grad_r2_low, sums2, upstream_stack, turned_upstream, delta = second_back(
        grad_r3, part, got, norm2_rows, normed2, inverse2, cross_out, recalled_full, top
    )
    upstream_stack, wide = barrier((upstream_stack, wide))
    wide = reduce_chips([wide], None)
    operands = (scales, scale_rows, upstream_stack, turned_queries, turned_upstream, delta)
    back = ()
    state_grads = []
    for base, spots, memory, powers in kept:
        heading = jnp.concatenate([jnp.stack([jnp.int32(base), core]), spots])
        *back, state_grad = cross_backward(heading, memory, powers, operands, back)
        state_grads.append(state_grad)
        if len(state_grads) == 2:
            near_states, back = barrier((near_states, back))
            near_pair = [near_states, exchange(near_states, "core")]
    wide, back = barrier((wide, back))
    wide = chip_sum(wide).astype(jnp.bfloat16)
    query_grad, value_bias_grad = back
    query_low, part, query_sums = query_back(query_grad, cross_query)
    got = swap_heads(part)

    def state_products(states, state_grads):
        total = 0.0
        for rows, state_grad in zip(states, state_grads):
            total = total + jnp.einsum(
                "ed,ke->dk", rows, state_grad, preferred_element_type=jnp.float32
            )
        return total

    near_pair, wide, part = barrier((near_pair, wide, part))
    wide = gather_plane(spread_depth(wide)[None])
    memory_grad = state_products(near_pair, state_grads[:2])
    got, memory_grad = barrier((got, memory_grad))
    grad_r1, grad_r1_low, sums1, grad_q, grad_k, grad_v, part, self_sums = self_back(
        grad_r2,
        part,
        got,
        norm1_rows,
        normed1,
        inverse1,
        self_out,
        queries,
        keys,
        values,
        attn,
        self_proj,
    )
    mine, sent = own_and_sent(even, decoder_in, grad_q, decoder_in, grad_v)
    mine_two, sent_two = own_and_sent(even, decoder_in, grad_k, grad_r1_low, mixed_low)
    self_keep = jnp.concatenate([mine, mine_two], axis=1)
    small = [
        self_sums[:2].reshape(1, MODEL),
        sums1[:3],
        jnp.concatenate([query_sums[:1], jnp.sum(value_bias_grad, axis=1)[None]], axis=1),
        sums2[:3],
        unit_sums[:1].reshape(2, MODEL),
        sums3[:3],
        jnp.zeros((3, MODEL), jnp.float32),
    ]
    terms = two_terms(jnp.concatenate(small, axis=0))
    self_sent = jnp.concatenate([sent, sent_two, ], axis=1)
    self_sent = jnp.concatenate([self_sent, terms], axis=0)
    got = exchange(self_sent, "core")
    input_grad = grad_r1 + (part.astype(jnp.float32) + swap_heads(part).astype(jnp.float32))

    far_states, self_sent = barrier((far_states, self_sent))
    far_pair = [far_states, exchange(far_states, "core")]
    memory_grad = memory_grad + state_products(far_pair, state_grads[2:])
    mine, sent = own_and_sent(even, after_self_low, query_low, grad_r2_low, recalled)
    cross_keep = jnp.concatenate([memory_grad[:, :WIDTH], mine], axis=1)
    cross_sent = jnp.concatenate([memory_grad[:, WIDTH:].astype(jnp.bfloat16), sent], axis=1)
    cross_got = exchange(cross_sent, "core")
    small = one_term(terms) + one_term(got[MODEL:])
    self_total = self_keep + got[:MODEL].astype(jnp.float32)
    cross_total = cross_keep + cross_got.astype(jnp.float32)
    cross_total, self_total, small, input_grad = barrier(
        (cross_total, self_total, small, input_grad)
    )
    chunks = reduce_chips([cross_total, self_total], small)

    rows = MODEL // CHIP_COUNT
    both_sum = chip_sum(chunks)
    lanes = MODEL // 2
    small = both_sum[2 * rows : 2 * rows + 1]
    small = two_terms(small[:, :lanes] + small[:, lanes:])
    piece = jnp.concatenate(
        [
            both_sum[: 2 * rows].astype(jnp.bfloat16),
            jnp.concatenate([small[:1], small[1:]], axis=1),
            jnp.zeros((EXTRA_ROWS - 1, MODEL), jnp.bfloat16),
        ],
        axis=0,
    )
    piece = spread_depth(piece)
    piece = spread_ring(piece, "b")
    wide, piece = barrier((wide, piece))
    wide = jnp.transpose(wide.reshape(RING, RING, 2, -1, MODEL), (0, 2, 1, 3, 4))
    five, six = by_core(wide.reshape(2 * MODEL, MODEL), even)
    grad_reduce = five.astype(jnp.float32)
    grad_expand = jnp.concatenate([six[:MODEL], six[MODEL:]], axis=1).astype(jnp.float32)
    mine = spread_ring(piece, "a")
    other = exchange(mine, "core")
    grad_cross_memory, grad_cross_query, grad_cross_out, grad_self_proj, grad_self_out = finish(
        core[None].astype(jnp.int32), mine, other
    )
    small = jnp.where(even, mine[:, :, :, 2 * rows], other[:, :, :, 2 * rows])
    small = jnp.transpose(small, (1, 2, 0, 3)).reshape(CHIP_COUNT, MODEL).astype(jnp.float32)
    small = (small[:, :lanes] + small[:, lanes:]).reshape(-1, MODEL)
    return (
        layer_out,
        input_grad,
        grad_self_proj,
        small[0].reshape(2, WIDTH),
        grad_self_out,
        small[1],
        small[2],
        small[3],
        grad_cross_query,
        grad_cross_memory,
        small[4].reshape(2, WIDTH),
        grad_cross_out,
        small[5],
        small[6],
        small[7],
        grad_expand,
        small[8:10].reshape(-1),
        grad_reduce,
        small[10],
        small[11],
        small[12],
    )


def solution(mesh):
    in_specs = (
        P(DP, None),
        P(DP, None),
        P(DP),
        P(DP, None),
        P(None, None, "head"),
        P(None, "head"),
        P("head", None),
        P(),
        P(),
        P(),
        P(None, "head"),
        P(None, None, "head"),
        P(None, "head"),
        P("head", None),
        P(),
        P(),
        P(),
        P(None, "head"),
        P("head"),
        P("head", None),
        P(),
        P(),
        P(),
        P(DP, None),
    )
    out_specs = (
        P(DP, None),
        P(DP, None),
        P(None, None, "head"),
        P(None, "head"),
        P("head", None),
        P(),
        P(),
        P(),
        P(None, "head"),
        P(None, None, "head"),
        P(None, "head"),
        P("head", None),
        P(),
        P(),
        P(),
        P(None, "head"),
        P("head"),
        P("head", None),
        P(),
        P(),
        P(),
    )
    grid = Mesh(mesh.devices.reshape(RING, 2, RING, 2, 2), DP + ("head",))
    return jax.shard_map(shards, mesh=grid, in_specs=in_specs, out_specs=out_specs, check_vma=False)
```

time: 1630 us -> 459 us (0.28)
  waiting for transfers between devices: 673 us -> 113 us
  blocking collectives: 416 us -> 0 us
  matrix products: 263 us -> 30.1 us
  Pallas kernels: 0 us -> 179 us
  local copies, waits for them, and re-layouts: 134 us -> 28.9 us
  other arithmetic: 108 us -> 26.1 us
  starting transfers between devices: 1.06 us -> 65.7 us
    psum x7 -> x0, waiting for transfers between devices: 481 us -> none  [the longest x1 372 us: shards(): lax.psum((grad_self_proj, grad_self_bias, grad_self_out, grad_self_out_bi...]
    psum x1 -> x0, blocking collectives: 318 us -> none  [shards(): lax.psum((grad_self_proj, grad_self_bias, grad_self_out, grad_self_out_bi...]
    dot_general x82 -> x16, matrix products: 261 us -> 30.1 us  [the longest x4 18.5 us: state_products(): jnp.einsum('ed,ke->dk', rows, state_grad, preferred_element_type=jnp.floa...]
    reduce_scatter x1 -> x0, waiting for transfers between devices: 191 us -> none  [shards(): lax.psum_scatter(state_parts, 'dp', scatter_dimension=0, tiled=True)]
    pallas_call x0 -> x18, Pallas kernels: none -> 179 us  [the longest x4 54.4 us: cross_backward(): pl.pallas_call(functools.partial(cross_backward_kernel, not running), gri...]
    all_gather x1 -> x0, blocking collectives: 97.9 us -> none  [shards(): lax.all_gather(keep_low, 'dp', axis=0, tiled=True)]
    ppermute x0 -> x30, waiting for transfers between devices: none -> 51.5 us  [the longest x6 23.3 us: swap_heads(): return lax.ppermute(part, 'head', [(0, 1), (1, 0)])]
    dynamic_slice x40 -> x0, local copies, waits for them, and re-layouts: 51.4 us -> none  [the longest x8 19.1 us: one_block(): value_block = lax.dynamic_slice_in_dim(value_piece, first_key, block_len, 0)]
  transfers between devices with their start and end apart: 10 -> 36, of which waited for: 6 -> 15; matrix products, arithmetic and copies ran while one was open for 8% -> 15% of each run, Pallas kernels for 0% -> 37%
where the time goes in v1:
time: 459 us; the launch traced here: 457 us
  Pallas kernels  179 us (39%)
  waiting for transfers between devices  113 us (25%)
  starting transfers between devices  65.7 us (14%)
  matrix products  30.1 us (7%)
  local copies, waits for them, and re-layouts  28.9 us (6%)
  other arithmetic  26.1 us (6%)
  between operations  15.5 us (3%)
    pallas_call x4, Pallas kernels, cross_backward(): pl.pallas_call(functools.partial(cross_backward_kernel, not running), gri...  54.4 us
    pallas_call x4, Pallas kernels, cross_forward(): pl.pallas_call(functools.partial(cross_forward_kernel, not running), grid...  48.7 us
    all_to_all x2, waiting for transfers between devices, reduce_chips(): lax.all_to_all(jnp.concatenate(chunks, axis=1), CHIPS, 0, 0, tiled=True)  40.5 us
    pallas_call x8, Pallas kernels, dense_call(): pl.pallas_call(kernel, in_specs=[pl.BlockSpec(memory_space=pltpu.VMEM)] *...  39.1 us
    pallas_call x1, Pallas kernels, selection_table(): pl.pallas_call(table_kernel, grid=(count // SEL_TOKENS,), in_specs=[pl.Bl...  29.2 us
    ppermute x6, waiting for transfers between devices, swap_heads(): return lax.ppermute(part, 'head', [(0, 1), (1, 0)])  23.3 us
    ppermute x12, waiting for transfers between devices, move_axis(): return lax.ppermute(array, DP, pairs)  22.9 us
    all_gather x4, waiting for transfers between devices, gather_plane(): return lax.all_gather(shard, ('y', 'x'), axis=0, tiled=True)  20.6 us
  transfers between devices with their start and end apart: 36, of which 15 were waited for; matrix products, arithmetic and copies ran while one was open for 15% of the time, Pallas kernels for 37%

profile of v1, /device:TPU:1, one launch (start us, length us, event | category | flops | bytes accessed | tf_op | source)
XLA Modules:
  0.0 457.4 jit_solution(6054855879928150002)
XLA Ops:
  24.4 29.2 %shard_map.392.refs_0_.refs_1_.refs_2_.refs_3_.refs_4_.refs_5_.refs_6_.refs_7_ = bf16[64,256,128]{2,1,0:T(8,128)(2,1)S(1)} custom-call(s32[256,1024]{1,0:T(8,128)S(1)} %copy-done.1), custom_call_target="tpu_custom_call" | custom-call | flops 1048576 | bytes 65536 | tf_op jit(solution)/shard_map/pallas_call | solution.py:63
  64.7 11.5 %all-gather.5.cloned.1.call-done = bf16[2304,768]{1,0:T(8,128)(2,1)} async-done(((bf16[144,768]{1,0:T(8,128)(2,1)}), bf16[2304,768]{1,0:T(8,128)(2,1)}) %all-gather.5.cloned.1.call-update) | async-done | bytes 3538960 | tf_op jit(solution)/shard_map/all_gather | solution.py:820
  77.2 11.4 %shard_map.394 = (bf16[2048,768]{1,0:T(8,128)(2,1)}, bf16[1536,2048]{1,0:T(8,128)(2,1)}, f32[1536,128]{1,0:T(8,128)}, f32[1536,128]{1,0:T(8,128)}, f32[1536,128]{1,0:T(8,128)}, /*index=5*/f32[1536,128]{1,0:T(8,128)}) custom-call(s32[17]{0:T(128)} %concatenate.128.slots, bf16[16,144,768]{2,1,0:T(8,128)(2,1)} %bitcast.138, bf16[64,256,128]{2,1,0:T(8,128)(2,1)} %copy-done, ...), custom_call_target="tpu_custom_call" | custom-call | flops 1048576 | bytes 65536 | tf_op jit(solution)/shard_map/pallas_call | solution.py:176
  96.8 12.4 %shard_map.395 = (bf16[2048,768]{1,0:T(8,128)(2,1)}, bf16[1536,2048]{1,0:T(8,128)(2,1)}, f32[1536,128]{1,0:T(8,128)}, f32[1536,128]{1,0:T(8,128)}, f32[1536,128]{1,0:T(8,128)}, /*index=5*/f32[1536,128]{1,0:T(8,128)}) custom-call(s32[17]{0:T(128)} %concatenate.132.slots, bf16[16,144,768]{2,1,0:T(8,128)(2,1)} %bitcast.71.rows_ref, ...), custom_call_target="tpu_custom_call" | custom-call | flops 1048576 | bytes 65536 | tf_op jit(solution)/shard_map/pallas_call | solution.py:176
  109.2 12.5 %shard_map.396 = (bf16[2048,768]{1,0:T(8,128)(2,1)}, bf16[1536,2048]{1,0:T(8,128)(2,1)}, f32[1536,128]{1,0:T(8,128)}, f32[1536,128]{1,0:T(8,128)}, f32[1536,128]{1,0:T(8,128)}, /*index=5*/f32[1536,128]{1,0:T(8,128)}) custom-call(s32[17]{0:T(128)} %pad_add_fusion.1.slots, bf16[16,144,768]{2,1,0:T(8,128)(2,1)} %bitcast.135, bf16[64,256,128]{2,1,0:T(8,128)(2,1)} %copy-done, ...), custom_call_target="tpu_custom_call" | custom-call | flops 1048576 | bytes 65536 | tf_op jit(solution)/shard_map/pallas_call | solution.py:176
  121.7 12.4 %shard_map.397 = (bf16[2048,768]{1,0:T(8,128)(2,1)}, bf16[1536,2048]{1,0:T(8,128)(2,1)}, f32[1536,128]{1,0:T(8,128)}, f32[1536,128]{1,0:T(8,128)}, f32[1536,128]{1,0:T(8,128)}, /*index=5*/f32[1536,128]{1,0:T(8,128)}) custom-call(s32[17]{0:T(128)} %pad_add_fusion.slots, bf16[16,144,768]{2,1,0:T(8,128)(2,1)} %bitcast.53.rows_ref, ...), custom_call_target="tpu_custom_call" | custom-call | flops 1048576 | bytes 65536 | tf_op jit(solution)/shard_map/pallas_call | solution.py:176
  137.8 12.3 %collective-permute-start.10 = (bf16[256,768]{1,0:T(8,128)(2,1)}, bf16[256,768]{1,0:T(8,128)(2,1)S(1)}, u32[]{:S(2)}, u32[]{:S(2)}) collective-permute-start(bf16[256,768]{1,0:T(8,128)(2,1)} %get-tuple-element.192.part_ref), channel_id=1, source_target_pairs={{0,1},{1,0},{2,3},{3,2},{4,5},{5,4},{6,7},{7,6},{8,9},{9,8},{10,11... | collective-permute-start | bytes 1179656 | tf_op jit(solution)/shard_map/ppermute | solution.py:915
  150.7 8.3 %collective-permute-done.10.got_ref = bf16[256,768]{1,0:T(8,128)(2,1)S(1)} collective-permute-done((bf16[256,768]{1,0:T(8,128)(2,1)}, bf16[256,768]{1,0:T(8,128)(2,1)S(1)}, u32[]{:S(2)}, u32[]{:S(2)}) %collective-permute-start.10) | collective-permute-done | bytes 393248 | tf_op jit(solution)/shard_map/ppermute | solution.py:915
  159.7 5.8 %shard_map.399 = (f32[256,768]{1,0:T(8,128)}, f32[256,768]{1,0:T(8,128)}, f32[256,128]{1,0:T(8,128)}, bf16[256,768]{1,0:T(8,128)(2,1)}, f32[256,1536]{1,0:T(8,12...) custom-call(f32[256,768]{1,0:T(8,128)} %get-tuple-element.163.after_ref, ...), custom_call_target="tpu_custom_call" | custom-call | flops 1048576 | bytes 65536 | tf_op jit(solution)/shard_map/pallas_call | solution.py:380
  166.8 7.9 %collective-permute-done.11.got_ref = bf16[256,768]{1,0:T(8,128)(2,1)S(1)} collective-permute-done((bf16[256,768]{1,0:T(8,128)(2,1)}, bf16[256,768]{1,0:T(8,128)(2,1)S(1)}, u32[]{:S(2)}, u32[]{:S(2)}) %collective-permute-start.11) | collective-permute-done | bytes 393248 | tf_op jit(solution)/shard_map/ppermute | solution.py:915
  175.5 6.7 %shard_map.400 = (bf16[256,768]{1,0:T(8,128)(2,1)}, f32[256,768]{1,0:T(8,128)}, bf16[256,768]{1,0:T(8,128)(2,1)}, bf16[256,1536]{1,0:T(8,128)(2,1)}, bf16[256,76...) custom-call(f32[256,768]{1,0:T(8,128)} %get-tuple-element.193.cross_ref, ...), custom_call_target="tpu_custom_call" | custom-call | flops 1048576 | bytes 65536 | tf_op jit(solution)/shard_map/pallas_call | solution.py:380
  191.7 7.1 %collective-permute-done.12.got_ref = bf16[256,768]{1,0:T(8,128)(2,1)S(1)} collective-permute-done((bf16[256,768]{1,0:T(8,128)(2,1)S(1)}, bf16[256,768]{1,0:T(8,128)(2,1)S(1)}, u32[]{:S(2)}, u32[]{:S(2)}) %collective-permute-start.12) | collective-permute-done | bytes 393248 | tf_op jit(solution)/shard_map/ppermute | solution.py:915
  207.7 13.3 %shard_map.402 = (f32[1536,128]{1,0:T(8,128)}, f32[384,128]{1,0:T(8,128)}, bf16[768,2048]{1,0:T(8,128)(2,1)}) custom-call(s32[18]{0:T(128)} %get-tuple-element.332.base_ref, bf16[2048,768]{1,0:T(8,128)(2,1)} %get-tuple-element.221.memory_ref, bf16[1536,2048]{1,0:T(8,128)(2,1)} %get-tuple-element.222.powers_ref, f32[1536,128]{1,0:T(8,128)} %get-tuple-element.210.scale_ref, ...), custom_call_target="tpu_custom_call" | custom-call | flops 1048576 | bytes 65536 | tf_op jit(solution)/shard_map/pallas_call | solution.py:295
  221.0 13.7 %shard_map.403 = (f32[1536,128]{1,0:T(8,128)}, f32[384,128]{1,0:T(8,128)}, bf16[768,2048]{1,0:T(8,128)(2,1)}) custom-call(s32[18]{0:T(128)} %get-tuple-element.331.base_ref, bf16[2048,768]{1,0:T(8,128)(2,1)} %get-tuple-element.219.memory_ref, bf16[1536,2048]{1,0:T(8,128)(2,1)} %get-tuple-element.220.powers_ref, f32[1536,128]{1,0:T(8,128)} %get-tuple-element.210.scale_ref, ...), custom_call_target="tpu_custom_call" | custom-call | flops 1048576 | bytes 65536 | tf_op jit(solution)/shard_map/pallas_call | solution.py:295
  235.5 9.1 %all-to-all-start = ((bf16[32,48,768]{2,1,0:T(8,128)(2,1)}), bf16[32,48,768]{2,1,0:T(8,128)(2,1)S(1)}, u32[]{:S(2)}, u32[]{:S(2)}) async-start(bf16[32,48,768]{2,1,0:T(8,128)(2,1)} %bitcast.134), calls=%async_computation | async-start | bytes 4718592 | tf_op jit(solution)/shard_map/all_to_all | solution.py:863
  246.1 13.7 %shard_map.404 = (f32[1536,128]{1,0:T(8,128)}, f32[384,128]{1,0:T(8,128)}, bf16[768,2048]{1,0:T(8,128)(2,1)}) custom-call(s32[18]{0:T(128)} %get-tuple-element.330.base_ref, bf16[2048,768]{1,0:T(8,128)(2,1)} %get-tuple-element.216.memory_ref, bf16[1536,2048]{1,0:T(8,128)(2,1)} %get-tuple-element.217.powers_ref, f32[1536,128]{1,0:T(8,128)} %get-tuple-element.210.scale_ref, ...), custom_call_target="tpu_custom_call" | custom-call | flops 1048576 | bytes 65536 | tf_op jit(solution)/shard_map/pallas_call | solution.py:295
  259.8 13.6 %shard_map.405 = (f32[1536,128]{1,0:T(8,128)}, f32[384,128]{1,0:T(8,128)}, bf16[768,2048]{1,0:T(8,128)(2,1)}) custom-call(s32[18]{0:T(128)} %get-tuple-element.329.base_ref, bf16[2048,768]{1,0:T(8,128)(2,1)} %get-tuple-element.208.memory_ref, bf16[1536,2048]{1,0:T(8,128)(2,1)} %get-tuple-element.209.powers_ref, f32[1536,128]{1,0:T(8,128)} %get-tuple-element.210.scale_ref, ...), custom_call_target="tpu_custom_call" | custom-call | flops 1048576 | bytes 65536 | tf_op jit(solution)/shard_map/pallas_call | solution.py:295
  282.5 5.6 %fusion.73 = f32[768,768]{1,0:T(8,128)S(1)} fusion(bf16[2048,768]{1,0:T(8,128)(2,1)} %collective-permute-done.15, bf16[768,2048]{1,0:T(8,128)(2,1)} %get-tuple-element.240), kind=kOutput, calls=%fused_computation.191 | convolution fusion | flops 2415919104 | bytes 8650752 | tf_op jit(solution)/shard_map/ed,ke->dk/dot_general | solution.py:1072
  291.6 7.9 %shard_map.407 = (f32[256,768]{1,0:T(8,128)}, bf16[256,768]{1,0:T(8,128)(2,1)}, f32[8,768]{1,0:T(8,128)}, bf16[256,384]{1,0:T(8,128)(2,1)}, bf16[256,384]{1,0:T(...) custom-call(f32[256,768]{1,0:T(8,128)} %get-tuple-element.243.grad_ref, ...), custom_call_target="tpu_custom_call" | custom-call | flops 1048576 | bytes 65536 | tf_op jit(solution)/shard_map/pallas_call | solution.py:380
  328.8 8.1 %all-to-all-start.1 = ((bf16[32,56,768]{2,1,0:T(8,128)(2,1)}), bf16[32,56,768]{2,1,0:T(8,128)(2,1)S(1)}, u32[]{:S(2)}, u32[]{:S(2)}) async-start(bf16[32,56,768]{2,1,0:T(8,128)(2,1)} %maximum_maximum_fusion), calls=%async_computation.1 | async-start | bytes 5505024 | tf_op jit(solution)/shard_map/all_to_all | solution.py:863
  337.6 37.0 %all-to-all-done.1 = bf16[32,56,768]{2,1,0:T(8,128)(2,1)S(1)} async-done(((bf16[32,56,768]{2,1,0:T(8,128)(2,1)}), bf16[32,56,768]{2,1,0:T(8,128)(2,1)S(1)}, u32[]{:S(2)}, u32[]{:S(2)}) %all-to-all-start.1) | async-done | bytes 2752544 | tf_op jit(solution)/shard_map/all_to_all | solution.py:863
  393.8 9.0 %all-gather.11.cloned.1.call-done = bf16[16,2,48,768]{3,2,1,0:T(8,128)(2,1)} async-done(((bf16[1,2,48,768]{3,2,1,0:T(8,128)(2,1)}), bf16[16,2,48,768]{3,2,1,0:T(8,128)(2,1)}) %all-gather.11.cloned.1.call-update) | async-done | bytes 2359312 | tf_op jit(solution)/shard_map/all_gather | solution.py:820
  415.0 7.3 %collective-permute-done.27 = bf16[4,2,56,768]{3,2,1,0:T(8,128)(2,1)} collective-permute-done((bf16[4,2,56,768]{3,2,1,0:T(8,128)(2,1)S(1)}, bf16[4,2,56,768]{3,2,1,0:T(8,128)(2,1)}, u32[]{:S(2)}, u32[]{:S(2)}) %collective-permute-start.27) | collective-permute-done | bytes 688160 | tf_op jit(solution)/shard_map/ppermute | solution.py:878
  443.6 7.1 %shard_map.408 = (f32[2,768,384]{2,1,0:T(8,128)}, f32[768,384]{1,0:T(8,128)}, f32[384,768]{1,0:T(8,128)}, f32[3,768,384]{2,1,0:T(8,128)}, f32[384,768]{1,0:T(8,128)}) custom-call(s32[1]{0:T(128)} %bitcast.73.core_ref, bf16[4,4,2,56,768]{4,3,2,1,0:T(8,128)(2,1)} %copy-done.2, bf16[4,4,2,56,768]{4,3,2,1,0:T(8,128)(2,1)} %copy-done.3, ...), custom_call_target="tpu_custom_call" | custom-call | flops 1048576 | bytes 65536 | tf_op jit(solution)/shard_map/pallas_call | solution.py:737
  (308 shorter events, 158.8 us)
Async XLA Ops:
  7.2 69.0 %all-gather.5.cloned.1.call-start = ((), (), s32[]{:S(2)}) async-start(), calls=%async_computation.2 | async-start | bytes 3760128 | tf_op jit(solution)/shard_map/all_gather | solution.py:820
  10.4 224.3 %all-gather.7.cloned.1.call-start = ((), (), s32[]{:S(2)}) async-start(), calls=%async_computation.3 | async-start | bytes 3342336 | tf_op jit(solution)/shard_map/all_gather | solution.py:820
  19.8 35.9 %collective-permute-start = (bf16[256,768]{1,0:T(8,128)(2,1)}, bf16[256,768]{1,0:T(8,128)(2,1)S(1)}, u32[]{:S(2)}, u32[]{:S(2)}) collective-permute-start(bf16[256,768]{1,0:T(8,128)(2,1)} %get-tuple-element.159.part_ref), channel_id=1, source_target_pairs={{0,1},{1,0},{2,3},{3,2},{4,5},{5,4},{6,7},{7,6},{8,9},{9,8},{10,11... | collective-permute-start | bytes 1179656 | tf_op jit(solution)/shard_map/ppermute | solution.py:915
  20.7 35.0 %collective-permute-start.2 = (bf16[144,768]{1,0:T(8,128)(2,1)S(1)}, bf16[144,768]{1,0:T(8,128)(2,1)S(1)}, u32[]{:S(2)}, u32[]{:S(2)}) collective-permute-start(bf16[144,768]{1,0:T(8,128)(2,1)S(1)} %pad_maximum_fusion.8), channel_id=1, source_target_pairs={{0,96},{2,14},{4,100},{6,2},{8,104},{10,6},{12,108},{14,10},{16,11... | collective-permute-start | bytes 663560 | tf_op jit(solution)/shard_map/ppermute | solution.py:878
  23.3 32.4 %collective-permute-start.3 = (bf16[144,768]{1,0:T(8,128)(2,1)S(1)}, bf16[144,768]{1,0:T(8,128)(2,1)S(1)}, u32[]{:S(2)}, u32[]{:S(2)}) collective-permute-start(bf16[144,768]{1,0:T(8,128)(2,1)S(1)} %pad_maximum_fusion.8), channel_id=1, source_target_pairs={{0,64},{2,10},{4,68},{6,14},{8,72},{10,2},{12,76},{14,6},{16,80},{... | collective-permute-start | bytes 663560 | tf_op jit(solution)/shard_map/ppermute | solution.py:878
  23.8 31.9 %collective-permute-start.4 = (bf16[144,768]{1,0:T(8,128)(2,1)S(1)}, bf16[144,768]{1,0:T(8,128)(2,1)S(1)}, u32[]{:S(2)}, u32[]{:S(2)}) collective-permute-start(bf16[144,768]{1,0:T(8,128)(2,1)S(1)} %pad_maximum_fusion.8), channel_id=1, source_target_pairs={{0,32},{2,6},{4,36},{6,10},{8,40},{10,14},{12,44},{14,2},{16,48},{... | collective-permute-start | bytes 663560 | tf_op jit(solution)/shard_map/ppermute | solution.py:878
  55.8 32.8 %collective-permute-start.5 = (bf16[576,768]{1,0:T(8,128)(2,1)S(1)}, bf16[576,768]{1,0:T(8,128)(2,1)S(1)}, u32[]{:S(2)}, u32[]{:S(2)}) collective-permute-start(bf16[576,768]{1,0:T(8,128)(2,1)S(1)} %constant_dynamic-update-slice_fusion), channel_id=1, source_target_pairs={{0,12},{2,98},{4,0},{6,102},{8,4},{10,106},{12,8},{14,110},{16,28}... | collective-permute-start | bytes 2654216 | tf_op jit(solution)/shard_map/ppermute | solution.py:878
  58.6 30.0 %collective-permute-start.6 = (bf16[576,768]{1,0:T(8,128)(2,1)S(1)}, bf16[576,768]{1,0:T(8,128)(2,1)S(1)}, u32[]{:S(2)}, u32[]{:S(2)}) collective-permute-start(bf16[576,768]{1,0:T(8,128)(2,1)S(1)} %constant_dynamic-update-slice_fusion), channel_id=1, source_target_pairs={{0,8},{2,66},{4,12},{6,70},{8,0},{10,74},{12,4},{14,78},{16,24},{1... | collective-permute-start | bytes 2654216 | tf_op jit(solution)/shard_map/ppermute | solution.py:878
  59.0 31.5 %collective-permute-start.7 = (bf16[576,768]{1,0:T(8,128)(2,1)S(1)}, bf16[576,768]{1,0:T(8,128)(2,1)}, u32[]{:S(2)}, u32[]{:S(2)}) collective-permute-start(bf16[576,768]{1,0:T(8,128)(2,1)S(1)} %constant_dynamic-update-slice_fusion), channel_id=1, source_target_pairs={{0,4},{2,34},{4,8},{6,38},{8,12},{10,42},{12,0},{14,46},{16,20},{1... | collective-permute-start | bytes 2654216 | tf_op jit(solution)/shard_map/ppermute | solution.py:878
  76.2 20.5 %collective-permute-start.9 = (bf16[2304,768]{1,0:T(8,128)(2,1)}, bf16[2304,768]{1,0:T(8,128)(2,1)}, u32[]{:S(2)}, u32[]{:S(2)}) collective-permute-start(bf16[2304,768]{1,0:T(8,128)(2,1)} %all-gather.5.cloned.1.call-done), channel_id=1, source_target_pairs={{0,2},{2,0},{4,6},{6,4},{8,10},{10,8},{12,14},{14,12},{16,18},{18,... | collective-permute-start | bytes 10616840 | tf_op jit(solution)/shard_map/ppermute | solution.py:801
  93.5 28.2 %collective-permute-start.8 = (bf16[2304,768]{1,0:T(8,128)(2,1)S(1)}, bf16[2304,768]{1,0:T(8,128)(2,1)}, u32[]{:S(2)}, u32[]{:S(2)}) collective-permute-start(bf16[2304,768]{1,0:T(8,128)(2,1)S(1)} %constant_dynamic-update-slice_fusion.4), channel_id=1, source_target_pairs={{0,2},{2,0},{4,6},{6,4},{8,10},{10,8},{12,14},{14,12},{16,18},{18,... | collective-permute-start | bytes 10616840 | tf_op jit(solution)/shard_map/ppermute | solution.py:801
  94.5 210.5 %all-gather.9.cloned.1.call-start = ((), (), s32[]{:S(2)}) async-start(), calls=%async_computation.4 | async-start | bytes 3342336 | tf_op jit(solution)/shard_map/all_gather | solution.py:820
  137.8 21.2 %collective-permute-start.10 = (bf16[256,768]{1,0:T(8,128)(2,1)}, bf16[256,768]{1,0:T(8,128)(2,1)S(1)}, u32[]{:S(2)}, u32[]{:S(2)}) collective-permute-start(bf16[256,768]{1,0:T(8,128)(2,1)} %get-tuple-element.192.part_ref), channel_id=1, source_target_pairs={{0,1},{1,0},{2,3},{3,2},{4,5},{5,4},{6,7},{7,6},{8,9},{9,8},{10,11... | collective-permute-start | bytes 1179656 | tf_op jit(solution)/shard_map/ppermute | solution.py:915
  184.8 19.3 %collective-permute-start.13 = (bf16[1536,768]{1,0:T(8,128)(2,1)S(1)}, bf16[1536,768]{1,0:T(8,128)(2,1)}, u32[]{:S(2)}, u32[]{:S(2)}) collective-permute-start(bf16[1536,768]{1,0:T(8,128)(2,1)S(1)} %pad_maximum_fusion.1), channel_id=1, source_target_pairs={{0,2},{2,0},{4,6},{6,4},{8,10},{10,8},{12,14},{14,12},{16,18},{18,... | collective-permute-start | bytes 7077896 | tf_op jit(solution)/shard_map/ppermute | solution.py:801
  234.7 47.8 %collective-permute-start.15 = (bf16[2048,768]{1,0:T(8,128)(2,1)}, bf16[2048,768]{1,0:T(8,128)(2,1)}, u32[]{:S(2)}, u32[]{:S(2)}) collective-permute-start(bf16[2048,768]{1,0:T(8,128)(2,1)} %all-gather.7.cloned.1.call-done), channel_id=1, source_target_pairs={{0,2},{2,0},{4,6},{6,4},{8,10},{10,8},{12,14},{14,12},{16,18},{18,... | collective-permute-start | bytes 9437192 | tf_op jit(solution)/shard_map/ppermute | solution.py:801
  235.5 41.3 %all-to-all-start = ((bf16[32,48,768]{2,1,0:T(8,128)(2,1)}), bf16[32,48,768]{2,1,0:T(8,128)(2,1)S(1)}, u32[]{:S(2)}, u32[]{:S(2)}) async-start(bf16[32,48,768]{2,1,0:T(8,128)(2,1)} %bitcast.134), calls=%async_computation | async-start | bytes 4718592 | tf_op jit(solution)/shard_map/all_to_all | solution.py:863
  305.0 12.2 %collective-permute-start.16 = (bf16[2048,768]{1,0:T(8,128)(2,1)}, bf16[2048,768]{1,0:T(8,128)(2,1)}, u32[]{:S(2)}, u32[]{:S(2)}) collective-permute-start(bf16[2048,768]{1,0:T(8,128)(2,1)} %all-gather.9.cloned.1.call-done), channel_id=1, source_target_pairs={{0,2},{2,0},{4,6},{6,4},{8,10},{10,8},{12,14},{14,12},{16,18},{18,... | collective-permute-start | bytes 9437192 | tf_op jit(solution)/shard_map/ppermute | solution.py:801
  309.5 16.1 %collective-permute-start.18 = (bf16[800,768]{1,0:T(8,128)(2,1)S(1)}, bf16[800,768]{1,0:T(8,128)(2,1)S(1)}, u32[]{:S(2)}, u32[]{:S(2)}) collective-permute-start(bf16[800,768]{1,0:T(8,128)(2,1)S(1)} %copy-done.9), channel_id=1, source_target_pairs={{0,2},{2,0},{4,6},{6,4},{8,10},{10,8},{12,14},{14,12},{16,18},{18,... | collective-permute-start | bytes 3686408 | tf_op jit(solution)/shard_map/ppermute | solution.py:801
  309.6 15.0 %collective-permute-start.19 = (bf16[256,768]{1,0:T(8,128)(2,1)S(1)}, bf16[256,768]{1,0:T(8,128)(2,1)S(1)}, u32[]{:S(2)}, u32[]{:S(2)}) collective-permute-start(bf16[256,768]{1,0:T(8,128)(2,1)S(1)} %copy-done.24), channel_id=1, source_target_pairs={{0,1},{1,0},{2,3},{3,2},{4,5},{5,4},{6,7},{7,6},{8,9},{9,8},{10,11... | collective-permute-start | bytes 1179656 | tf_op jit(solution)/shard_map/ppermute | solution.py:915
  323.7 13.2 %collective-permute-start.20 = (bf16[48,768]{1,0:T(8,128)(2,1)S(1)}, bf16[48,768]{1,0:T(8,128)(2,1)S(1)}, u32[]{:S(2)}, u32[]{:S(2)}) collective-permute-start(bf16[48,768]{1,0:T(8,128)(2,1)S(1)} %copy-done.31), channel_id=1, source_target_pairs={{0,16},{2,18},{4,20},{6,22},{8,24},{10,26},{12,28},{14,30},{16,0},... | collective-permute-start | bytes 221192 | tf_op jit(solution)/shard_map/ppermute | solution.py:801
  328.8 45.8 %all-to-all-start.1 = ((bf16[32,56,768]{2,1,0:T(8,128)(2,1)}), bf16[32,56,768]{2,1,0:T(8,128)(2,1)S(1)}, u32[]{:S(2)}, u32[]{:S(2)}) async-start(bf16[32,56,768]{2,1,0:T(8,128)(2,1)} %maximum_maximum_fusion), calls=%async_computation.1 | async-start | bytes 5505024 | tf_op jit(solution)/shard_map/all_to_all | solution.py:863
  336.8 66.0 %all-gather.11.cloned.1.call-start = ((), (), s32[]{:S(2)}) async-start(), calls=%async_computation.5 | async-start | bytes 2506752 | tf_op jit(solution)/shard_map/all_gather | solution.py:820
  403.8 18.5 %collective-permute-start.27 = (bf16[4,2,56,768]{3,2,1,0:T(8,128)(2,1)S(1)}, bf16[4,2,56,768]{3,2,1,0:T(8,128)(2,1)}, u32[]{:S(2)}, u32[]{:S(2)}) collective-permute-start(bf16[4,2,56,768]{3,2,1,0:T(8,128)(2,1)S(1)} %pad_maximum_fusion.7), channel_id=1, source_target_pairs={{0,4},{2,34},{4,8},{6,38},{8,12},{10,42},{12,0},{14,46},{16,20},{1... | collective-permute-start | bytes 2064392 | tf_op jit(solution)/shard_map/ppermute | solution.py:878
  406.4 21.5 %collective-permute-start.29 = (bf16[1536,768]{1,0:T(8,128)(2,1)S(1)}, bf16[1536,768]{1,0:T(8,128)(2,1)}, u32[]{:S(2)}, u32[]{:S(2)}) collective-permute-start(bf16[1536,768]{1,0:T(8,128)(2,1)S(1)} %bitcast.133), channel_id=1, source_target_pairs={{0,2},{2,0},{4,6},{6,4},{8,10},{10,8},{12,14},{14,12},{16,18},{18,... | collective-permute-start | bytes 7077896 | tf_op jit(solution)/shard_map/ppermute | solution.py:801
  (69 other events, 711.1 us)
Sparse Core Ops, SparseCore 0:
  10.8 65.4 all-gather.4
  94.6 47.7 all-gather.6
  188.2 47.3 all-gather.8
  340.1 62.7 all-gather.10
